TPU v7x, 32 devices: a whole 2x2x4 slice. The times are simulated.
32 devices in a mesh: gx: 4 (over x, core), gy: 8 (over z, y).
Axes of the slice: x: 2, y: 2, z: 4, core: 2. Of those that a mesh axis runs over, the one named last changes fastest.
Arguments:
- blocks: float32 [4096, 4, 4096], P(('gx', 'gy')), may hold values from -0.75 to 0.75
- prolong: float32 [4096, 4096], P(('gx', 'gy')), may hold values from -2 to 2
- columns: int32 [4096, 4], P(('gx', 'gy')), may hold values from 0 to 4095, as said below
- aggregate: int32 [4096], P(('gx', 'gy')), may hold values from 0 to 2047, as said below
- column_slot: int32 [4096, 4], P(('gx', 'gy')), may hold values from 0 to 6, as said below
- owner_row: int32 [2048], P(('gx', 'gy')), may hold values from 0 to 2047, as said below
Outputs:
- merged_panel: float32 [4096, 7, 4096], P(('gx', 'gy'))
Inputs may be any that keep to these rules, and one draw needn't show every extreme that they name: `columns`: row i lists i first, then 3 distinct other blocks within 3 of i. `aggregate`: fine rows 4p+2 to 4p+5 (mod 4096) form coarse rows 2p and 2p+1 in that order, the first taking 1 to 3 of them. column_slot[i, k] = (aggregate[columns[i, k]] - aggregate[i] + 3) mod 2048. `owner_row`: a permutation. Coarse row I is held by device I // 64 and stored on device owner_row[I] // 64, a device with the same gy index; every device stores exactly 64 rows, and at most 17 of the rows held by one device go to one device, a bound reached in every draw.
All inputs are finite; a program needn't handle non-finite values.
Results may differ from a plain program's by a relative error of at most 0.0003.
Values sent between devices are 32-bit elements; how exact they have to be, the bound alone decides.
No kernel may reach another device: no remote copies, remote signals or barrier semaphores. Data moves between devices by JAX's collectives and lax.ppermute only.
A program may use at most 192 MiB of HBM per device.

v0:
```python
import jax
import jax.numpy as jnp
from jax import lax
from jax.sharding import PartitionSpec as P

BS = 64
NNZ = 4
REACH = 3
SLOTS = 7


def extended_2(cells, sides, width):
    for axis, dim in sides:
        count = lax.axis_size(axis)
        ends = count - 1
        head = lax.slice_in_dim(cells, 0, width, axis=dim)
        tail = lax.slice_in_dim(cells, cells.shape[dim] - width, cells.shape[dim], axis=dim)
        cells = jnp.concatenate(
            [
                lax.ppermute(tail, axis, [(i, (i + 1) % count) for i in range(ends)]),
                cells,
                lax.ppermute(head, axis, [((i + 1) % count, i) for i in range(ends)]),
            ],
            axis=dim,
        )
    return cells


def passed_along(value, axis, steps):
    count = lax.axis_size(axis)
    pairs = [(source, (source + steps) % count) for source in range(count)]
    return lax.ppermute(value, axis, pairs)


def partner_2(value, axis, apart):
    mask = 2**apart
    pairs = [(source, source ^ mask) for source in range(lax.axis_size(axis))]
    return lax.ppermute(value, axis, pairs)


def galerkin_terms(block_rows, left_blocks, right_blocks):
    count = block_rows.shape[0]
    matrix = block_rows.reshape(count, NNZ, BS, BS)
    left_q = left_blocks.reshape(count, BS, BS)
    right_q = right_blocks.reshape(count, NNZ, BS, BS)
    product = jnp.einsum("ikab,ikbc->ikac", matrix, right_q, precision=lax.Precision.HIGHEST)
    sandwich = jnp.einsum("iba,ikbc->ikac", left_q, product, precision=lax.Precision.HIGHEST)
    return sandwich.reshape(count * NNZ, BS * BS)


def bucket(row_data, owners, local_slot, size_gx, size_gy, home_count, capacity, panel_rows):
    dest_gx = owners // home_count // size_gy
    onehot = (dest_gx[:, None] == jnp.arange(size_gx, dtype=jnp.int32)[None, :]).astype(jnp.int32)
    rank_in = jnp.sum((jnp.cumsum(onehot, axis=0) - onehot) * onehot, axis=1)
    slot_index = dest_gx * capacity + rank_in
    buffer = (
        jnp.zeros((size_gx * capacity,) + row_data.shape[1:], row_data.dtype)
        .at[slot_index]
        .set(row_data)
    )
    labels = jnp.full((size_gx * capacity,), panel_rows, jnp.int32).at[slot_index].set(local_slot)
    return (
        buffer.reshape((size_gx, capacity) + row_data.shape[1:]),
        labels.reshape(size_gx, capacity),
    )


def land(received, labels, panel_rows):
    flattened = received.reshape((-1,) + received.shape[2:])
    landed = jnp.zeros((panel_rows + 1,) + flattened.shape[1:], flattened.dtype)
    return landed.at[labels.reshape(-1)].set(flattened)[:panel_rows]


def body(blocks, prolong, columns, aggregate, column_slot, owner_row):
    fine_rows = blocks.shape[0]
    home_count = fine_rows // 2
    block_area = BS * BS
    size_gx = lax.axis_size("gx")
    size_gy = lax.axis_size("gy")
    coarse_total = home_count * size_gx * size_gy
    capacity = home_count // size_gx + 1
    position = lax.axis_index(("gx", "gy"))
    first_block = position * fine_rows
    extended = extended_2(prolong, ((("gx", "gy"), 0),), REACH)
    near_index = columns - first_block + REACH
    right_blocks = extended[near_index]
    slot_row = jnp.remainder(aggregate - position * home_count + 2, coarse_total)
    values = galerkin_terms(blocks, prolong, right_blocks)
    target = ((slot_row - 0)[:, None] * SLOTS + column_slot).reshape(-1)
    all_terms = jax.ops.segment_sum(values, target, num_segments=(home_count + 2) * SLOTS)
    edge_terms = all_terms[: 2 * SLOTS]
    remaining = all_terms[2 * SLOTS :]
    incoming = passed_along(edge_terms, ("gx", "gy"), -1)
    home_rows = (
        remaining.at[(home_count - 2) * SLOTS :]
        .add(incoming)
        .reshape(home_count, SLOTS, block_area)
    )
    lower_half = lax.axis_index("gy") % 2 == 0
    buffer, labels = bucket(
        home_rows,
        owner_row,
        owner_row % home_count,
        size_gx,
        size_gy,
        home_count,
        capacity,
        home_count,
    )
    received, got_labels = (
        lax.all_to_all(buffer, "gx", split_axis=0, concat_axis=0, tiled=True),
        lax.all_to_all(labels, "gx", split_axis=0, concat_axis=0, tiled=True),
    )
    owner_panel = land(received, got_labels, home_count)
    partner = partner_2(owner_panel, "gy", 0)
    merged = jnp.where(
        lower_half,
        jnp.concatenate([owner_panel, partner], axis=0),
        jnp.concatenate([partner, owner_panel], axis=0),
    )
    return merged


def solution(mesh):
    placed = (
        P(("gx", "gy"), None, None),
        P(("gx", "gy"), None),
        P(("gx", "gy"), None),
        P(("gx", "gy")),
        P(("gx", "gy"), None),
        P(("gx", "gy")),
    )
    return jax.shard_map(
        body, mesh=mesh, in_specs=placed, out_specs=P(("gx", "gy"), None, None), check_vma=False
    )
```

profile of v0, /device:TPU:0, one launch (start us, length us, event | category | flops | bytes accessed | tf_op | source)
XLA Modules:
  0.0 552.1 jit_solution(525714531852662232)
XLA Ops:
  0.0 1.0 fusion.13
  1.0 4.9 collective-permute-start
  5.9 1.3 collective-permute-start.1
  7.2 0.7 compare_select_fusion
  7.9 0.1 copy.16
  8.0 0.1 reshape.96
  8.1 0.7 and_select_fusion.1
  8.8 0.7 fusion.8
  9.5 0.7 broadcast_add_fusion
  10.2 1.9 copy.20
  12.1 10.0 %copy.17 = f32[128,4,4096]{0,2,1:T(8,128)} copy(f32[128,4,4096]{2,1,0:T(4,128)} %param.8) | data formatting | bytes 16777216 | tf_op args[0]
  22.1 16.2 %copy.19 = f32[128,4,64,64]{3,2,1,0:T(8,128)} copy(f32[128,4,64,64]{0,3,2,1:T(8,128)} %bitcast.22) | data formatting | bytes 16777216 | tf_op jit(solution)/shard_map/reshape | solution.py:43
  38.4 4.5 copy.28
  42.9 0.1 copy.15
  43.2 1.8 pad_maximum_fusion
  45.1 5.2 gather_fusion
  50.3 14.2 %reshape.87 = f32[128,4,64,64]{3,2,1,0:T(8,128)} reshape(f32[512,4096]{1,0:T(8,128)} %gather_fusion) | data formatting | bytes 16777216 | tf_op jit(solution)/shard_map/reshape | solution.py:45
  64.5 32.9 %fusion.14 = f32[128,4,64,64]{3,2,1,0:T(8,128)S(1)} fusion(f32[128,4,64,64]{3,2,1,0:T(8,128)} %reshape.87, f32[128,4,64,64]{3,2,1,0:T(8,128)} %copy.19), kind=kOutput, calls=%fused_computation.39 | convolution fusion | flops 1610612736 | bytes 25165824 | tf_op jit(solution)/shard_map/ikab,ikbc->ikac/dot_general | solution.py:46
  97.5 17.4 %fusion.2 = f32[128,4,64,64]{2,3,1,0:T(8,128)} fusion(f32[128,64,64,1]{2,1,3,0:T(8,128)S(1)} %copy-done.2, f32[128,4,64,64]{3,2,1,0:T(8,128)S(1)} %fusion.14), kind=kOutput, calls=%fused_computation.8 | convolution fusion | flops 1610612736 | bytes 18874368 | tf_op jit(solution)/shard_map/iba,ikbc->ikac/dot_general | solution.py:47
  114.8 17.5 %copy.22 = f32[128,4,64,64]{3,2,1,0:T(8,128)} copy(f32[128,4,64,64]{2,3,1,0:T(8,128)} %fusion.2) | data formatting | bytes 16777216 | tf_op jit(solution)/shard_map/iba,ikbc->ikac/transpose | solution.py:47
  132.3 14.7 %reshape.114 = f32[512,4096]{1,0:T(8,128)} reshape(f32[128,4,64,64]{3,2,1,0:T(8,128)} %copy.22) | data formatting | bytes 16777216 | tf_op jit(solution)/shard_map/reshape | solution.py:48
  147.0 17.8 %scatter_custom_fusion.1 = f32[462,4096]{1,0:T(8,128)} fusion(s32[512]{0:T(512)S(1)} %reshape.112, f32[512,4096]{1,0:T(8,128)} %reshape.114, f32[]{:T(128)} %constant.111.clone.1), kind=kCustom, calls=%fused_computation.9 | custom fusion | flops 2097152 | bytes 7569920 | tf_op jit(solution)/shard_map/scatter-add | solution.py:90
  164.8 1.0 slice.45
  165.8 5.5 %collective-permute-start.2 = (f32[14,4096]{1,0:T(8,128)S(1)}, f32[14,4096]{1,0:T(8,128)S(1)}, u32[]{:S(2)}, u32[]{:S(2)}) collective-permute-start(f32[14,4096]{1,0:T(8,128)S(1)} %slice.45), channel_id=1, source_target_pairs={{0,31},{1,0},{2,1},{3,2},{4,3},{5,4},{6,5},{7,6},{8,7},{9,8},{10,9... | collective-permute-start | bytes 688136 | tf_op jit(solution)/shard_map/ppermute | solution.py:32
  171.4 0.2 select_reduce_fusion
  171.5 0.8 scatter_custom_fusion
  172.3 0.7 all_to_all.9
  173.0 3.3 all-to-all-start
  176.3 7.4 %slice.43 = f32[448,4096]{1,0:T(8,128)} slice(f32[462,4096]{1,0:T(8,128)} %scatter_custom_fusion.1), slice={[14:462], [0:4096]} | slice | bytes 14680064 | tf_op jit(solution)/shard_map/slice | solution.py:92
  183.7 1.0 slice_add_fusion
  184.7 1.7 scatter-add.13
  186.4 6.9 %reshape.122 = f32[64,7,4096]{2,1,0:T(8,128)} reshape(f32[448,4096]{1,0:T(8,128)} %scatter-add.13) | data formatting | bytes 14680064 | tf_op jit(solution)/shard_map/reshape | solution.py:97
  193.3 4.7 broadcast_in_dim.26
  198.0 16.0 %scatter_fusion = f32[68,7,4096]{2,1,0:T(8,128)} fusion(f32[68,7,4096]{2,1,0:T(8,128)} %broadcast_in_dim.26, s32[64]{0:T(128)S(1)} %compare_select_fusion.2, f32[64,7,4096]{2,1,0:T(8,128)} %reshape.122), kind=kCustom, calls=%fused_computation.3 | custom fusion | bytes 22020352 | tf_op jit(solution)/shard_map/scatter | solution.py:59
  213.9 5.7 %all-to-all-start.1 = ((f32[4,17,7,4096]{3,2,1,0:T(8,128)}), f32[4,17,7,4096]{3,2,1,0:T(8,128)}, u32[]{:S(2)}, u32[]{:S(2)}) async-start(f32[4,17,7,4096]{3,2,1,0:T(8,128)} %bitcast.21), calls=%async_computation.1 | async-start | bytes 17825792 | tf_op jit(solution)/shard_map/all_to_all | solution.py:111
  219.7 0.5 broadcast.90
  220.2 0.7 reduce.5
  221.0 97.5 %all-to-all-done.1 = f32[4,17,7,4096]{3,2,1,0:T(8,128)} async-done(((f32[4,17,7,4096]{3,2,1,0:T(8,128)}), f32[4,17,7,4096]{3,2,1,0:T(8,128)}, u32[]{:S(2)}, u32[]{:S(2)}) %all-to-all-start.1) | async-done | bytes 7798816 | tf_op jit(solution)/shard_map/all_to_all | solution.py:111
  318.5 4.5 broadcast_in_dim.23
  323.0 19.5 %scatter_fusion.1 = f32[65,7,4096]{2,1,0:T(8,128)} fusion(f32[65,7,4096]{2,1,0:T(8,128)} %broadcast_in_dim.23, s32[68]{0:T(128)S(1)} %fusion.10, f32[68,7,4096]{2,1,0:T(8,128)} %bitcast.8), kind=kCustom, calls=%fused_computation.4 | custom fusion | bytes 23396624 | tf_op jit(solution)/shard_map/scatter | solution.py:71
  342.5 3.9 slice.46
  346.4 3.4 copy-done
  349.8 7.2 %copy.23 = f32[64,7,4096]{2,0,1:T(8,128)} copy(f32[64,7,4096]{2,1,0:T(8,128)S(1)} %slice.46) | data formatting | bytes 14680064 | tf_op jit(solution)/shard_map/slice | solution.py:71
  357.0 0.6 collective-permute-start.3
  357.6 159.2 %collective-permute-done.3 = f32[64,7,4096]{2,0,1:T(8,128)} collective-permute-done((f32[64,7,4096]{2,0,1:T(8,128)}, f32[64,7,4096]{2,0,1:T(8,128)}, u32[]{:S(2)}, u32[]{:S(2)}) %collective-permute-start.3) | collective-permute-done | bytes 7340064 | tf_op jit(solution)/shard_map/ppermute | solution.py:38
  516.9 7.4 %copy.24 = f32[64,7,4096]{2,1,0:T(8,128)S(1)} copy(f32[64,7,4096]{2,0,1:T(8,128)} %collective-permute-done.3) | data formatting | bytes 14680064 | tf_op jit(solution)/shard_map/ppermute | solution.py:38
  524.3 7.8 %maximum_select_fusion = f32[128,7,4096]{2,1,0:T(8,128)} fusion(f32[64,7,4096]{2,1,0:T(8,128)S(1)} %copy.24, f32[64,7,4096]{2,1,0:T(8,128)S(1)} %copy-done.1, pred[]{:T(512)S(6)} %eq.22), kind=kLoop, calls=%fused_computation.5 | loop fusion | flops 11010048 | bytes 29360128 | tf_op jit(solution)/shard_map/jit(_where)/select_n | solution.py:116
  532.1 19.7 %copy.26 = f32[128,7,4096]{2,0,1:T(8,128)} copy(f32[128,7,4096]{2,1,0:T(8,128)} %maximum_select_fusion) | data formatting | bytes 29360128 | tf_op jit(solution)/shard_map/jit(_where)/select_n | solution.py:116
  (16 shorter events, 0.4 us)
Async XLA Ops:
  1.0 42.2 %collective-permute-start = (f32[3,4096]{1,0:T(4,128)S(1)}, f32[3,4096]{1,0:T(4,128)S(1)}, u32[]{:S(2)}, u32[]{:S(2)}) collective-permute-start(f32[3,4096]{1,0:T(4,128)S(1)} %get-tuple-element.17), channel_id=1, source_target_pairs={{0,1},{1,2},{2,3},{3,4},{4,5},{5,6},{6,7},{7,8},{8,9},{9,10},{10,1... | collective-permute-start | bytes 147464 | tf_op jit(solution)/shard_map/ppermute | solution.py:20
  5.9 37.4 %collective-permute-start.1 = (f32[3,4096]{1,0:T(4,128)S(1)}, f32[3,4096]{1,0:T(4,128)S(1)}, u32[]{:S(2)}, u32[]{:S(2)}) collective-permute-start(f32[3,4096]{1,0:T(4,128)S(1)} %get-tuple-element.18), channel_id=1, source_target_pairs={{1,0},{2,1},{3,2},{4,3},{5,4},{6,5},{7,6},{8,7},{9,8},{10,9},{11,1... | collective-permute-start | bytes 147464 | tf_op jit(solution)/shard_map/ppermute | solution.py:22
  64.5 33.0 %copy-start.2 = (f32[128,64,64,1]{2,1,3,0:T(8,128)S(1)}, f32[128,64,64,1]{2,1,3,0:T(8,128)}, u32[]{:S(2)}) copy-start(f32[128,64,64,1]{2,1,3,0:T(8,128)} %copy.28) | copy-start | bytes 6291460
  165.8 17.9 %collective-permute-start.2 = (f32[14,4096]{1,0:T(8,128)S(1)}, f32[14,4096]{1,0:T(8,128)S(1)}, u32[]{:S(2)}, u32[]{:S(2)}) collective-permute-start(f32[14,4096]{1,0:T(8,128)S(1)} %slice.45), channel_id=1, source_target_pairs={{0,31},{1,0},{2,1},{3,2},{4,3},{5,4},{6,5},{7,6},{8,7},{9,8},{10,9... | collective-permute-start | bytes 688136 | tf_op jit(solution)/shard_map/ppermute | solution.py:32
  173.0 41.0 %all-to-all-start = ((s32[4,1,17]{2,1,0:T(1,128)}), s32[4,1,17]{2,1,0:T(1,128)S(1)}, u32[]{:S(2)}, u32[]{:S(2)}) async-start(s32[4,1,17]{2,1,0:T(1,128)} %bitcast), calls=%async_computation | async-start | bytes 4096 | tf_op jit(solution)/shard_map/all_to_all | solution.py:112
  213.9 104.6 %all-to-all-start.1 = ((f32[4,17,7,4096]{3,2,1,0:T(8,128)}), f32[4,17,7,4096]{3,2,1,0:T(8,128)}, u32[]{:S(2)}, u32[]{:S(2)}) async-start(f32[4,17,7,4096]{3,2,1,0:T(8,128)} %bitcast.21), calls=%async_computation.1 | async-start | bytes 17825792 | tf_op jit(solution)/shard_map/all_to_all | solution.py:111
  346.4 3.4 copy-start
  357.0 159.9 %collective-permute-start.3 = (f32[64,7,4096]{2,0,1:T(8,128)}, f32[64,7,4096]{2,0,1:T(8,128)}, u32[]{:S(2)}, u32[]{:S(2)}) collective-permute-start(f32[64,7,4096]{2,0,1:T(8,128)} %copy.23), channel_id=1, source_target_pairs={{0,1},{1,0},{2,3},{3,2},{4,5},{5,4},{6,7},{7,6},{8,9},{9,8},{10,11... | collective-permute-start | bytes 22020104 | tf_op jit(solution)/shard_map/ppermute | solution.py:38
  357.6 166.6 %copy-start.1 = (f32[64,7,4096]{2,1,0:T(8,128)S(1)}, f32[64,7,4096]{2,1,0:T(8,128)}, u32[]{:S(2)}) copy-start(f32[64,7,4096]{2,1,0:T(8,128)} %copy-done) | copy-start | bytes 22020100
where the time goes:
time: 559 us; the launch traced here: 552 us
  waiting for transfers between devices  257 us (46%)
  local copies, waits for them, and re-layouts  191 us (34%)
  matrix products  50.3 us (9%)
  other arithmetic  32.2 us (6%)
  starting transfers between devices  21.4 us (4%)
    ppermute x1, waiting for transfers between devices, partner_2(): return lax.ppermute(value, axis, pairs)  159 us
    all_to_all x1, waiting for transfers between devices, body(): lax.all_to_all(buffer, 'gx', split_axis=0, concat_axis=0, tiled=True)  97.5 us
    dot_general x1, matrix products, galerkin_terms(): jnp.einsum('ikab,ikbc->ikac', matrix, right_q, precision=lax.Precision.HI...  32.9 us
    select_n x1, local copies, waits for them, and re-layouts, body(): jnp.where(lower_half, jnp.concatenate([owner_panel, partner], axis=0), jn...  19.7 us
    scatter x1, local copies, waits for them, and re-layouts, land(): return landed.at[labels.reshape(-1)].set(flattened)[:panel_rows]  19.5 us
    scatter-add x1, other arithmetic, body(): jax.ops.segment_sum(values, target, num_segments=(home_count + 2) * SLOTS)  17.8 us
    transpose x1, local copies, waits for them, and re-layouts, galerkin_terms(): jnp.einsum('iba,ikbc->ikac', left_q, product, precision=lax.Precision.HIG...  17.5 us
    dot_general x1, matrix products, galerkin_terms(): jnp.einsum('iba,ikbc->ikac', left_q, product, precision=lax.Precision.HIG...  17.4 us
  transfers between devices with their start and end apart: 6, of which 2 were waited for; matrix products, arithmetic and copies ran while one was open for 14% of the time, Pallas kernels for 0%

commit v1 on v0

v1 whole, which is shorter than its diff:
```python
import functools

import jax
import jax.numpy as jnp
from jax import lax
from jax.experimental import pallas as pl
from jax.experimental.pallas import tpu as pltpu
from jax.sharding import PartitionSpec as P

BS = 64
NNZ = 4
SLOTS = 7
ROW_BLOCKS = 6
MOST_FINE = 3
LANES = 128
PACK = BS * BS // LANES
BEFORE = 1
LABEL_ROWS = 8
GROUP = 4
ROW_BITS = 10

F32 = jnp.float32
BF16 = jnp.bfloat16
ANY = pl.BlockSpec(memory_space=pl.ANY)
SMEM = pl.BlockSpec(memory_space=pltpu.SMEM)
VMEM = pl.BlockSpec(memory_space=pltpu.VMEM)


def half_lanes(shape):
    return lax.broadcasted_iota(jnp.int32, shape, 1) < LANES // 2


def turned(value):
    return pltpu.roll(value, LANES // 2, 1)


def split(value):
    high = value.astype(BF16)
    low = (value - high.astype(F32)).astype(BF16)
    return high, low


def prepare_kernel(fine_rows, q_ref, before_ref, after_ref, w_ref, t_ref, natural, flipped):
    left = half_lanes((PACK, LANES))
    left_tall = half_lanes((BS, LANES))

    def one(source, base, window, lane, fine):
        packed = source[pl.ds(base, PACK, stride=8), :]
        swapped = turned(packed)
        even = jnp.where(left, packed, swapped)
        odd = jnp.where(left, swapped, packed)
        natural[lane, pl.ds(0, PACK, stride=2), :] = even
        natural[lane, pl.ds(1, PACK, stride=2), :] = odd
        high, low = split(natural[lane])
        w_ref[window, 0:BS, :] = high
        w_ref[window, BS : 2 * BS, :] = low
        if fine is not None:
            stacked = jnp.concatenate([even, odd, even, odd], axis=0)
            flipped[lane] = stacked.T[0:BS]
            ordered = jnp.concatenate(
                [flipped[lane, pl.ds(0, PACK, stride=2), :], flipped[lane, pl.ds(1, PACK, stride=2), :]], axis=0
            )
            high, low = split(ordered)
            t_ref[fine] = jnp.where(left_tall, high.astype(F32), low.astype(F32)).astype(BF16)

    @pl.loop(0, fine_rows // 8)
    def _(group):
        for lane in range(8):
            row = group * 8 + lane
            one(q_ref, group * (8 * PACK) + lane, row + BEFORE, lane, row)

    one(before_ref, 7, 0, 0, None)
    for row in range(5):
        one(after_ref, row, fine_rows + BEFORE + row, row, fine_rows + row if row < 2 else None)


def bucket_kernel(
    shift,
    fine_rows,
    fine_total,
    home_count,
    rows_of_gx,
    capacity,
    most,
    me_ref,
    columns_ref,
    slots_ref,
    aggregate_ref,
    owner_ref,
    edge_ref,
    blocks_ref,
    edge_blocks_ref,
    w_ref,
    t_ref,
    token_ref,
    out_ref,
    stored,
    total,
    label_ref,
    fine_list,
    window_list,
    place_list,
    place_of,
    in_sem,
    out_sem,
):
    wanted = me_ref[0] ^ shift
    first_block = me_ref[1] * fine_rows
    flat = lax.broadcasted_iota(jnp.int32, (LABEL_ROWS, LANES), 0) * LANES + lax.broadcasted_iota(
        jnp.int32, (LABEL_ROWS, LANES), 1
    )

    def edge_or(ref, row, offset, k=None):
        own = row < fine_rows
        inside = jnp.where(own, row, 0)
        outside = jnp.where(own, 0, row - fine_rows)
        if k is None:
            return jnp.where(own, ref[inside], edge_ref[offset + outside])
        return jnp.where(own, ref[k, inside], edge_ref[offset + k * 2 + outside])

    def fetch(row, index):
        target = stored.at[pl.ds(pl.multiple_of(index * 2 * BS, 2 * BS), 2 * BS)]

        @pl.when(row < fine_rows)
        def _():
            pltpu.make_async_copy(blocks_ref.at[row], target, in_sem).start()

        @pl.when(row >= fine_rows)
        def _():
            pltpu.make_async_copy(edge_blocks_ref.at[row - fine_rows], target, in_sem).start()

    def coarse_row(local, carry):
        used, listed, labels = carry
        owner = owner_ref[local]
        match = owner // rows_of_gx == wanted
        start = (local // 2) * 4 + 2
        leading = edge_or(aggregate_ref, start, 4 * NNZ)
        size = (
            1
            + (edge_or(aggregate_ref, start + 1, 4 * NNZ) == leading).astype(jnp.int32)
            + (edge_or(aggregate_ref, start + 2, 4 * NNZ) == leading).astype(jnp.int32)
        )
        second = local % 2 == 1
        first_fine = jnp.where(second, start + size, start)
        count = jnp.where(second, 4 - size, size)
        for slot in range(SLOTS):
            place_of[slot] = -1

        def fine_row(step, inner):
            used, listed, labels = inner
            row = first_fine + step
            fetch(row, listed)
            fine_list[listed] = row
            for k in range(NNZ):
                slot = edge_or(slots_ref, row, 2 * NNZ, k)
                window = edge_or(columns_ref, row, 0, k) - first_block + BEFORE
                window = jnp.where(window < 0, window + fine_total, window)
                window = jnp.where(window >= fine_total, window - fine_total, window)
                seen = place_of[slot]
                new = seen < 0
                place = jnp.where(new, used, seen)
                place_of[slot] = place
                used = used + new.astype(jnp.int32)
                label = (slot * 2**ROW_BITS + owner % home_count).astype(F32)
                labels = jnp.where(flat == place, label, labels)
                window_list[listed * NNZ + k] = window
                place_list[listed * NNZ + k] = place
            return used, listed + 1, labels

        return lax.fori_loop(0, jnp.where(match, count, 0), fine_row, (used, listed, labels))

    used, listed, labels = lax.fori_loop(
        0, home_count, coarse_row, (jnp.int32(0), jnp.int32(0), jnp.zeros((LABEL_ROWS, LANES), F32))
    )
    label_ref[...] = jnp.where(flat == LABEL_ROWS * LANES - 1, used.astype(F32), labels)
    label_out = pltpu.make_async_copy(label_ref, out_ref.at[pl.ds(capacity * PACK, LABEL_ROWS)], out_sem.at[1])
    label_out.start()
    groups = (listed + GROUP - 1) // GROUP

    def filler(index, _):
        fine_list[index] = 0
        for k in range(NNZ):
            window_list[index * NNZ + k] = 0
            place_list[index * NNZ + k] = most
        return 0

    lax.fori_loop(listed, groups * GROUP, filler, 0)

    @pl.loop(0, most + 1)
    def _(place):
        total[pl.ds(pl.multiple_of(place * PACK, PACK), PACK), :] = jnp.zeros((PACK, LANES), F32)

    @pl.loop(0, listed)
    def _(index):
        pltpu.make_async_copy(blocks_ref.at[0], stored.at[pl.ds(0, 2 * BS)], in_sem).wait()

    left = half_lanes((PACK, LANES))
    left_tall = half_lanes((BS, LANES))

    @pl.loop(0, groups)
    def _(group):
        results = []
        for lane in range(GROUP):
            index = group * GROUP + lane
            products = []
            for k in range(NNZ):
                packed = stored[pl.ds(index * 2 * BS + k, PACK, stride=NNZ), :]
                high = packed.astype(BF16).astype(F32)
                low = packed - high
                even = jnp.where(left, high, turned(low))
                odd = jnp.where(left, turned(high), low)
                both = jnp.concatenate([even, odd], axis=0).astype(BF16)
                factor = w_ref[window_list[index * NNZ + k]]
                q_high = factor[0:BS]
                q_low = factor[BS : 2 * BS]
                products.append(
                    jnp.dot(
                        jnp.concatenate([both, both], axis=1),
                        jnp.concatenate([q_high, q_high, q_low, q_low], axis=0),
                        preferred_element_type=F32,
                    )
                )
            wide = jnp.concatenate(
                [
                    jnp.where(left_tall, products[0], products[1]),
                    jnp.where(left_tall, products[2], products[3]),
                ],
                axis=1,
            )
            high, low = split(wide)
            row = t_ref[fine_list[index]]
            results.append(
                jnp.dot(
                    jnp.concatenate([row, row], axis=1),
                    jnp.concatenate([high, high, low, low], axis=0),
                    preferred_element_type=F32,
                )
            )
        for lane in range(GROUP):
            index = group * GROUP + lane
            for pair in range(2):
                even = results[lane][0:PACK, pair * LANES : (pair + 1) * LANES]
                odd = results[lane][PACK:BS, pair * LANES : (pair + 1) * LANES]
                packed = [jnp.where(left, even, turned(odd)), jnp.where(left, turned(even), odd)]
                for k in range(2):
                    place = place_list[index * NNZ + pair * 2 + k]
                    where = pl.ds(pl.multiple_of(place * PACK, PACK), PACK)
                    total[where, :] = total[where, :] + packed[k]

    main_out = pltpu.make_async_copy(
        total.at[pl.ds(0, capacity * PACK)], out_ref.at[pl.ds(0, capacity * PACK)], out_sem.at[0]
    )
    main_out.start()
    main_out.wait()
    label_out.wait()


def place_kernel(counts, capacity, home_count, clear, me_ref, *refs):
    own_count, partner_count = counts
    sources = refs[: own_count + partner_count]
    rest = refs[own_count + partner_count :]
    out_ref, labels, zeros, label_sem, zero_sem, sem = rest[-6:]
    slots, row_groups = out_ref.shape[0], out_ref.shape[1]
    copies = []
    for which, source in enumerate(sources):
        copies.append(
            pltpu.make_async_copy(
                source.at[pl.ds(capacity * PACK, LABEL_ROWS)], labels.at[which], label_sem.at[which]
            )
        )
        copies[-1].start()
    if clear:
        zeros[...] = jnp.zeros_like(zeros)

        @pl.loop(0, slots)
        def _(slot):
            @pl.loop(0, row_groups)
            def _(group):
                pltpu.make_async_copy(zeros, out_ref.at[slot, group], zero_sem).start()

        @pl.loop(0, slots * row_groups)
        def _(step):
            pltpu.make_async_copy(zeros, out_ref.at[0, 0], zero_sem).wait()

    moved = jnp.int32(0)
    for which, source in enumerate(sources):
        copies[which].wait()
        upper = me_ref[2] if which < own_count else 1 - me_ref[2]
        used = labels[which, LABEL_ROWS - 1, 0, LANES - 1].astype(jnp.int32)

        @pl.loop(0, used)
        def _(place):
            label = labels[which, place // LANES, 0, place % LANES].astype(jnp.int32)
            slot = label // 2**ROW_BITS
            row = label % 2**ROW_BITS + upper * home_count
            pltpu.make_async_copy(
                source.at[pl.ds(place * PACK, PACK)], out_ref.at[slot, row // 8, :, row % 8], sem
            ).start()

        moved = moved + used

    @pl.loop(0, moved)
    def _(step):
        pltpu.make_async_copy(sources[0].at[pl.ds(0, PACK)], out_ref.at[0, 0, :, 0], sem).wait()


def placed_into(out, out_type, me, own, partner, capacity, home_count):
    sources = [value.reshape(-1, 1, LANES) for value in own + partner]
    clear = out is None
    return pl.pallas_call(
        functools.partial(place_kernel, (len(own), len(partner)), capacity, home_count, clear),
        in_specs=[SMEM] + [ANY] * (len(sources) + (0 if clear else 1)),
        out_specs=ANY,
        out_shape=out_type,
        input_output_aliases={} if clear else {len(sources) + 1: 0},
        scratch_shapes=[
            pltpu.SMEM((len(sources), LABEL_ROWS, 1, LANES), F32),
            pltpu.VMEM((PACK, 8, 1, LANES), F32),
            pltpu.SemaphoreType.DMA((len(sources),)),
            pltpu.SemaphoreType.DMA,
            pltpu.SemaphoreType.DMA,
        ],
        compiler_params=pltpu.CompilerParams(vmem_limit_bytes=32 * 2**20),
    )(me, *sources, *([] if clear else [out]))


def body(blocks, prolong, columns, aggregate, column_slot, owner_row):
    fine_rows = blocks.shape[0]
    home_count = owner_row.shape[0]
    size_gx = lax.axis_size("gx")
    size_gy = lax.axis_size("gy")
    size = size_gx * size_gy
    here_gx = lax.axis_index("gx")
    here_gy = lax.axis_index("gy")
    position = lax.axis_index(("gx", "gy"))
    most = (home_count // size_gx + 1) * ROW_BLOCKS
    capacity = most
    most_fine = -(-(home_count // size_gx + 1) * MOST_FINE // GROUP) * GROUP
    me = jnp.stack([here_gx, position, here_gy % 2]).astype(jnp.int32)

    block_view = (
        blocks.reshape(fine_rows, NNZ, PACK, LANES).transpose(0, 2, 1, 3).reshape(fine_rows, NNZ * PACK, LANES)
    )
    q_view = (
        prolong.reshape(fine_rows // 8, 8, PACK, LANES).transpose(0, 2, 1, 3).reshape(fine_rows * PACK, LANES)
    )
    group_rows = 8 * PACK
    backward = [(i, (i - 1) % size) for i in range(size)]
    forward = [(i, (i + 1) % size) for i in range(size)]
    axes = ("gx", "gy")
    edge_ints = jnp.concatenate(
        [columns.T[:, :2].reshape(-1), column_slot.T[:, :2].reshape(-1), aggregate[:2]]
    )
    edge_ints = lax.ppermute(edge_ints, axes, backward)
    after = lax.ppermute(q_view[:group_rows], axes, backward)
    edge_blocks = lax.ppermute(block_view[:2], axes, backward)
    before = lax.ppermute(q_view[-group_rows:], axes, forward)

    right, left = pl.pallas_call(
        functools.partial(prepare_kernel, fine_rows),
        in_specs=[VMEM] * 3,
        out_specs=[VMEM] * 2,
        out_shape=[
            jax.ShapeDtypeStruct((fine_rows + BEFORE + 5, 2 * BS, LANES), BF16),
            jax.ShapeDtypeStruct((fine_rows + 2, BS, LANES), BF16),
        ],
        scratch_shapes=[pltpu.VMEM((8, BS, LANES), F32), pltpu.VMEM((8, BS, LANES), F32)],
        compiler_params=pltpu.CompilerParams(vmem_limit_bytes=32 * 2**20),
    )(q_view, before, after)

    def bucket(shift, token):
        return pl.pallas_call(
            functools.partial(
                bucket_kernel,
                shift,
                fine_rows,
                fine_rows * size,
                home_count,
                home_count * size_gy,
                capacity,
                most,
            ),
            in_specs=[SMEM] * 6 + [ANY] * 2 + [VMEM] * 2 + [ANY],
            out_specs=ANY,
            out_shape=jax.ShapeDtypeStruct((capacity * PACK + LABEL_ROWS, LANES), F32),
            scratch_shapes=[
                pltpu.VMEM((most_fine * 2 * BS, LANES), F32),
                pltpu.VMEM(((most + 1) * PACK, LANES), F32),
                pltpu.VMEM((LABEL_ROWS, LANES), F32),
                pltpu.SMEM((most_fine,), jnp.int32),
                pltpu.SMEM((most_fine * NNZ,), jnp.int32),
                pltpu.SMEM((most_fine * NNZ,), jnp.int32),
                pltpu.SMEM((8,), jnp.int32),
                pltpu.SemaphoreType.DMA,
                pltpu.SemaphoreType.DMA((2,)),
            ],
            compiler_params=pltpu.CompilerParams(vmem_limit_bytes=40 * 2**20),
        )(
            me,
            columns.T,
            column_slot.T,
            aggregate,
            owner_row,
            edge_ints,
            block_view,
            edge_blocks,
            right,
            left,
            token,
        )

    def across(value, shift):
        pairs = [(source, source ^ shift) for source in range(size_gx)]
        return lax.ppermute(value, "gx", pairs)

    def partner(value):
        pairs = [(source, source ^ 1) for source in range(size_gy)]
        return lax.ppermute(value, "gy", pairs)

    own_sent = bucket(0, me)
    own_partner = partner(own_sent)
    arrived = []
    token = own_sent
    for shift in list(range(2, size_gx)) + [1]:
        sent = bucket(shift, token)
        token = sent
        arrived.append(across(sent, shift))
    arrived = arrived[-1:] + arrived[:-1]
    from_partner = [partner(value) for value in arrived]

    out_type = jax.ShapeDtypeStruct((SLOTS, 2 * home_count // 8, PACK, 8, 1, LANES), F32)
    common = (out_type, me)
    limits = (capacity, home_count)
    out = placed_into(None, *common, [own_sent] + arrived, [], *limits)
    out = placed_into(out, *common, [], [own_partner, from_partner[0]], *limits)
    for value in from_partner[1:]:
        out = placed_into(out, *common, [], [value], *limits)
    return (
        out.reshape(SLOTS, 2 * home_count // 8, PACK, 8, LANES)
        .transpose(1, 3, 0, 2, 4)
        .reshape(2 * home_count, SLOTS, BS * BS)
    )


def solution(mesh):
    placed = (
        P(("gx", "gy"), None, None),
        P(("gx", "gy"), None),
        P(("gx", "gy"), None),
        P(("gx", "gy")),
        P(("gx", "gy"), None),
        P(("gx", "gy")),
    )
    return jax.shard_map(
        body, mesh=mesh, in_specs=placed, out_specs=P(("gx", "gy"), None, None), check_vma=False
    )
```

time: 559 us -> 235 us (0.42); the launches traced: 552 us -> 235 us
  local copies, waits for them, and re-layouts: 191 us -> 5.08 us
  waiting for transfers between devices: 257 us -> 124 us
  Pallas kernels: 0 us -> 89.9 us
  matrix products: 50.3 us -> 0 us
  other arithmetic: 32.2 us -> 0.81 us
  starting transfers between devices: 21.4 us -> 14.4 us
    all_to_all x2 -> x0, waiting for transfers between devices: 97.5 us -> none  [the longest x1 97.5 us: body(): lax.all_to_all(buffer, 'gx', split_axis=0, concat_axis=0, tiled=True)]
    pallas_call x0 -> x9, Pallas kernels: none -> 89.9 us  [the longest x4 57.9 us: bucket(): pl.pallas_call(functools.partial(bucket_kernel, shift, fine_rows, fine_ro...]
    reshape x6 -> x2, local copies, waits for them, and re-layouts: 56.7 us -> 1.53 us  [the longest x1 0.76 us: body(): column_slot.T[:, :2].reshape(-1)]
    dot_general x2 -> x0, matrix products: 50.3 us -> none  [the longest x1 32.9 us: galerkin_terms(): jnp.einsum('ikab,ikbc->ikac', matrix, right_q, precision=lax.Precision.HI...]
    scatter x3 -> x0, local copies, waits for them, and re-layouts: 36.2 us -> none  [the longest x1 19.5 us: land(): return landed.at[labels.reshape(-1)].set(flattened)[:panel_rows]]
    ppermute x4 -> x11, waiting for transfers between devices: 159 us -> 124 us  [the longest x3 72.2 us: across(): return lax.ppermute(value, 'gx', pairs)]
    select_n x2 -> x0, local copies, waits for them, and re-layouts: 19.8 us -> none  [the longest x1 19.7 us: body(): jnp.where(lower_half, jnp.concatenate([owner_panel, partner], axis=0), jn...]
    slice x5 -> x2, local copies, waits for them, and re-layouts: 20.5 us -> 1.95 us  [the longest x1 0.99 us: body(): after = lax.ppermute(q_view[:group_rows], axes, backward)]
  transfers between devices with their start and end apart: 6 -> 11, of which waited for: 2 -> 6; matrix products, arithmetic and copies ran while one was open for 14% -> 1% of each run, Pallas kernels for 0% -> 12%
where the time goes in v1:
time: 235 us
  waiting for transfers between devices  124 us (53%)
  Pallas kernels  89.9 us (38%)
  starting transfers between devices  14.4 us (6%)
  local copies, waits for them, and re-layouts  5.08 us (2%)
    ppermute x3, waiting for transfers between devices, across(): return lax.ppermute(value, 'gx', pairs)  72.2 us
    pallas_call x4, Pallas kernels, bucket(): pl.pallas_call(functools.partial(bucket_kernel, shift, fine_rows, fine_ro...  57.9 us
    ppermute x4, waiting for transfers between devices, partner(): return lax.ppermute(value, 'gy', pairs)  50.5 us
    pallas_call x4, Pallas kernels, placed_into(): pl.pallas_call(functools.partial(place_kernel, (len(own), len(partner)),...  26.9 us
    ppermute x1, starting transfers between devices, body(): edge_blocks = lax.ppermute(block_view[:2], axes, backward)  6.43 us
    pallas_call x1, Pallas kernels, body(): pl.pallas_call(functools.partial(prepare_kernel, fine_rows), in_specs=[VM...  5.11 us
  transfers between devices with their start and end apart: 11, of which 6 were waited for; matrix products, arithmetic and copies ran while one was open for 1% of the time, Pallas kernels for 12%

profile of v1, /device:TPU:0, one launch (start us, length us, event | category | flops | bytes accessed | tf_op | source)
XLA Modules:
  0.0 234.5 jit_solution(1144958326193221358)
XLA Ops:
  0.0 0.0 copy-start.1
  0.0 0.0 copy-start.2
  0.0 0.0 copy-start.3
  0.0 0.0 copy-start.4
  0.0 1.0 slice.36
  1.0 6.4 %collective-permute-start.1 = (f32[2,128,128]{2,1,0:T(8,128)S(1)}, f32[2,128,128]{2,1,0:T(8,128)S(1)}, u32[]{:S(2)}, u32[]{:S(2)}) collective-permute-start(f32[2,128,128]{2,1,0:T(8,128)S(1)} %bitcast.68), channel_id=1, source_target_pairs={{0,31},{1,0},{2,1},{3,2},{4,3},{5,4},{6,5},{7,6},{8,7},{9,8},{10,9... | collective-permute-start | bytes 393224 | tf_op jit(solution)/shard_map/ppermute | solution.py:356
  7.4 1.0 slice_bitcast_fusion
  8.4 0.3 collective-permute-start.3
  8.7 1.8 collective-permute-start.2
  10.5 0.8 reshape.51
  11.2 0.8 reshape.52
  12.0 0.7 pad_add_fusion.1
  12.7 3.5 %collective-permute-start = (s32[18]{0:T(128)S(1)}, s32[18]{0:T(128)S(1)}, u32[]{:S(2)}, u32[]{:S(2)}) collective-permute-start(s32[18]{0:T(128)S(1)} %pad_add_fusion.1), channel_id=1, source_target_pairs={{0,31},{1,0},{2,1},{3,2},{4,3},{5,4},{6,5},{7,6},{8,7},{9,8},{10,9... | collective-permute-start | bytes 224 | tf_op jit(solution)/shard_map/ppermute | solution.py:354
  16.3 0.1 pad_add_fusion.me_ref.token_ref
  16.4 0.0 collective-permute-done.3.after_ref
  16.4 1.5 collective-permute-done.2.before_ref
  17.8 0.0 copy-start
  17.8 1.6 copy-done
  19.4 5.1 %shard_map.64 = (bf16[134,128,128]{2,1,0:T(8,128)(2,1)S(1)}, bf16[130,64,128]{2,1,0:T(8,128)(2,1)S(1)}) custom-call(f32[4096,128]{1,0:T(8,128)S(1)} %bitcast.44, f32[256,128]{1,0:T(8,128)S(1)} %collective-permute-done.2.before_ref, f32[256,128]{1,0:T(8,128)S(1)} %collective-permute-done.3.after_ref), custom_call_target="tpu_custom_call" | custom-call | tf_op jit(solution)/shard_map/pallas_call | solution.py:359
  24.5 0.0 collective-permute-done.edge_ref
  24.5 0.0 collective-permute-done.1.edge_blocks_ref
  24.5 0.0 copy-done.1
  24.6 0.0 copy-done.2
  24.6 0.0 copy-done.3
  24.6 0.0 copy-done.4
  24.6 12.8 %shard_map.65.token_ref = f32[3272,128]{1,0:T(8,128)S(1)} custom-call(s32[3]{0:T(128)S(1)} %pad_add_fusion.me_ref.token_ref, s32[4,128]{1,0:T(4,128)S(1)} %bitcast.53, s32[4,128]{1,0:T(4,128)S(1)} %bitcast.58, s32[128]{0:T(128)S(1)} %copy-done.3, s32[64]{0:T(128)S(1)} %copy-done.4, s32[18]{0:T(128)S(1)} %collective-permute-done.edge_ref, ...), custom_call_target="tpu_custom_call" | custom-call | tf_op jit(solution)/shard_map/pallas_call | solution.py:372
  37.4 14.1 %shard_map.66.token_ref = f32[3272,128]{1,0:T(8,128)S(1)} custom-call(s32[3]{0:T(128)S(1)} %pad_add_fusion.me_ref.token_ref, s32[4,128]{1,0:T(4,128)S(1)} %bitcast.54, s32[4,128]{1,0:T(4,128)S(1)} %bitcast.59, s32[128]{0:T(128)S(1)} %copy-done.3, s32[64]{0:T(128)S(1)} %copy-done.4, s32[18]{0:T(128)S(1)} %collective-permute-done.edge_ref, ...), custom_call_target="tpu_custom_call" | custom-call | tf_op jit(solution)/shard_map/pallas_call | solution.py:372
  51.6 14.3 %shard_map.67.token_ref = f32[3272,128]{1,0:T(8,128)S(1)} custom-call(s32[3]{0:T(128)S(1)} %pad_add_fusion.me_ref.token_ref, s32[4,128]{1,0:T(4,128)S(1)} %bitcast.55, s32[4,128]{1,0:T(4,128)S(1)} %bitcast.60, s32[128]{0:T(128)S(1)} %copy-done.3, s32[64]{0:T(128)S(1)} %copy-done.4, s32[18]{0:T(128)S(1)} %collective-permute-done.edge_ref, ...), custom_call_target="tpu_custom_call" | custom-call | tf_op jit(solution)/shard_map/pallas_call | solution.py:372
  65.9 16.6 %shard_map.68 = f32[3272,128]{1,0:T(8,128)S(1)} custom-call(s32[3]{0:T(128)S(1)} %pad_add_fusion.me_ref.token_ref, s32[4,128]{1,0:T(4,128)S(1)} %bitcast.56, s32[4,128]{1,0:T(4,128)S(1)} %bitcast.61, s32[128]{0:T(128)S(1)} %copy-done.3, s32[64]{0:T(128)S(1)} %copy-done.4, s32[18]{0:T(128)S(1)} %collective-permute-done.edge_ref, f32[128,128,128]{2,1,0:T(8,128)} %bitcast.67, ...), custom_call_target="tpu_custom_call" | custom-call | tf_op jit(solution)/shard_map/pallas_call | solution.py:372
  82.5 0.1 collective-permute-start.9
  82.6 1.7 collective-permute-start.6
  84.3 0.2 collective-permute-start.4
  84.4 0.0 collective-permute-start.8
  84.4 1.7 collective-permute-done.9
  86.1 0.3 collective-permute-start.10
  86.5 35.6 %collective-permute-done.6 = f32[3272,128]{1,0:T(8,128)S(1)} collective-permute-done((f32[3272,128]{1,0:T(8,128)S(1)}, f32[3272,128]{1,0:T(8,128)S(1)}, u32[]{:S(2)}, u32[]{:S(2)}) %collective-permute-start.6) | collective-permute-done | bytes 1675296 | tf_op jit(solution)/shard_map/ppermute | solution.py:414
  122.0 0.0 collective-permute-start.7
  122.0 35.0 %collective-permute-done.4 = f32[3272,128]{1,0:T(8,128)S(1)} collective-permute-done((f32[3272,128]{1,0:T(8,128)S(1)}, f32[3272,128]{1,0:T(8,128)S(1)}, u32[]{:S(2)}, u32[]{:S(2)}) %collective-permute-start.4) | collective-permute-done | bytes 1675296 | tf_op jit(solution)/shard_map/ppermute | solution.py:414
  157.0 0.0 collective-permute-start.5
  157.0 14.4 %shard_map.69.refs_2_ = f32[7,16,32,8,1,128]{5,4,3,2,1,0:T(1,128)} custom-call(s32[3]{0:T(128)S(1)} %pad_add_fusion.me_ref.token_ref, f32[3272,1,128]{2,1,0:T(1,128)S(1)} %bitcast.42, f32[3272,1,128]{2,1,0:T(1,128)S(1)} %bitcast.49, f32[3272,1,128]{2,1,0:T(1,128)S(1)} %bitcast.48, f32[3272,1,128]{2,1,0:T(1,128)S(1)} %bitcast.47), custom_call_target="tpu_custom_call" | custom-call | tf_op jit(solution)/shard_map/pallas_call | solution.py:310
  171.4 0.0 collective-permute-done.8
  171.4 0.0 collective-permute-done.10
  171.4 5.4 %shard_map.70.refs_1_ = f32[7,16,32,8,1,128]{5,4,3,2,1,0:T(1,128)} custom-call(s32[3]{0:T(128)S(1)} %pad_add_fusion.me_ref.token_ref, f32[3272,1,128]{2,1,0:T(1,128)S(1)} %bitcast.45, f32[3272,1,128]{2,1,0:T(1,128)S(1)} %bitcast.46, f32[7,16,32,8,1,128]{5,4,3,2,1,0:T(1,128)} %shard_map.69.refs_2_), custom_call_target="tpu_custom_call", output_to_operand_aliasing={{}: (3, {})} | custom-call | tf_op jit(solution)/shard_map/pallas_call | solution.py:310
  176.9 18.8 %collective-permute-done.7 = f32[3272,128]{1,0:T(8,128)S(1)} collective-permute-done((f32[3272,128]{1,0:T(8,128)S(1)}, f32[3272,128]{1,0:T(8,128)S(1)}, u32[]{:S(2)}, u32[]{:S(2)}) %collective-permute-start.7) | collective-permute-done | bytes 1675296 | tf_op jit(solution)/shard_map/ppermute | solution.py:418
  195.6 3.5 %shard_map.71.refs_1_ = f32[7,16,32,8,1,128]{5,4,3,2,1,0:T(1,128)} custom-call(s32[3]{0:T(128)S(1)} %pad_add_fusion.me_ref.token_ref, f32[3272,1,128]{2,1,0:T(1,128)S(1)} %bitcast.50, f32[7,16,32,8,1,128]{5,4,3,2,1,0:T(1,128)} %shard_map.70.refs_1_), custom_call_target="tpu_custom_call", output_to_operand_aliasing={{}: (2, {})} | custom-call | tf_op jit(solution)/shard_map/pallas_call | solution.py:310
  199.2 31.8 %collective-permute-done.5 = f32[3272,128]{1,0:T(8,128)S(1)} collective-permute-done((f32[3272,128]{1,0:T(8,128)S(1)}, f32[3272,128]{1,0:T(8,128)S(1)}, u32[]{:S(2)}, u32[]{:S(2)}) %collective-permute-start.5) | collective-permute-done | bytes 1675296 | tf_op jit(solution)/shard_map/ppermute | solution.py:418
  231.0 3.5 %shard_map.72 = f32[7,16,32,8,1,128]{5,4,3,2,1,0:T(1,128)} custom-call(s32[3]{0:T(128)S(1)} %pad_add_fusion.me_ref.token_ref, f32[3272,1,128]{2,1,0:T(1,128)S(1)} %bitcast.51, f32[7,16,32,8,1,128]{5,4,3,2,1,0:T(1,128)} %shard_map.71.refs_1_), custom_call_target="tpu_custom_call", output_to_operand_aliasing={{}: (2, {})} | custom-call | tf_op jit(solution)/shard_map/pallas_call | solution.py:310
Async XLA Ops:
  0.0 24.5 %copy-start.1 = (s32[128,4]{0,1:T(4,128)S(1)}, s32[128,4]{0,1:T(4,128)}, u32[]{:S(2)}) copy-start(s32[128,4]{0,1:T(4,128)} %param.8) | copy-start | bytes 6148
  0.0 24.6 %copy-start.2 = (s32[128,4]{0,1:T(4,128)S(1)}, s32[128,4]{0,1:T(4,128)}, u32[]{:S(2)}) copy-start(s32[128,4]{0,1:T(4,128)} %param.10) | copy-start | bytes 6148
  0.0 24.6 %copy-start.3 = (s32[128]{0:T(128)S(1)}, s32[128]{0:T(128)}, u32[]{:S(2)}) copy-start(s32[128]{0:T(128)} %aggregate_ref.7) | copy-start | bytes 1540
  0.0 24.6 %copy-start.4 = (s32[64]{0:T(128)S(1)}, s32[64]{0:T(128)}, u32[]{:S(2)}) copy-start(s32[64]{0:T(128)} %owner_ref.7) | copy-start | bytes 772
  1.0 23.6 %collective-permute-start.1 = (f32[2,128,128]{2,1,0:T(8,128)S(1)}, f32[2,128,128]{2,1,0:T(8,128)S(1)}, u32[]{:S(2)}, u32[]{:S(2)}) collective-permute-start(f32[2,128,128]{2,1,0:T(8,128)S(1)} %bitcast.68), channel_id=1, source_target_pairs={{0,31},{1,0},{2,1},{3,2},{4,3},{5,4},{6,5},{7,6},{8,7},{9,8},{10,9... | collective-permute-start | bytes 393224 | tf_op jit(solution)/shard_map/ppermute | solution.py:356
  8.4 8.0 %collective-permute-start.3 = (f32[256,128]{1,0:T(8,128)S(1)}, f32[256,128]{1,0:T(8,128)S(1)}, u32[]{:S(2)}, u32[]{:S(2)}) collective-permute-start(f32[256,128]{1,0:T(8,128)S(1)} %get-tuple-element.9), channel_id=1, source_target_pairs={{0,31},{1,0},{2,1},{3,2},{4,3},{5,4},{6,5},{7,6},{8,7},{9,8},{10,9... | collective-permute-start | bytes 393224 | tf_op jit(solution)/shard_map/ppermute | solution.py:355
  8.7 9.2 %collective-permute-start.2 = (f32[256,128]{1,0:T(8,128)S(1)}, f32[256,128]{1,0:T(8,128)S(1)}, u32[]{:S(2)}, u32[]{:S(2)}) collective-permute-start(f32[256,128]{1,0:T(8,128)S(1)} %get-tuple-element.10), channel_id=1, source_target_pairs={{0,1},{1,2},{2,3},{3,4},{4,5},{5,6},{6,7},{7,8},{8,9},{9,10},{10,1... | collective-permute-start | bytes 393224 | tf_op jit(solution)/shard_map/ppermute | solution.py:357
  12.7 11.8 %collective-permute-start = (s32[18]{0:T(128)S(1)}, s32[18]{0:T(128)S(1)}, u32[]{:S(2)}, u32[]{:S(2)}) collective-permute-start(s32[18]{0:T(128)S(1)} %pad_add_fusion.1), channel_id=1, source_target_pairs={{0,31},{1,0},{2,1},{3,2},{4,3},{5,4},{6,5},{7,6},{8,7},{9,8},{10,9... | collective-permute-start | bytes 224 | tf_op jit(solution)/shard_map/ppermute | solution.py:354
  17.8 1.6 copy-start
  82.5 3.6 %collective-permute-start.9 = (f32[3272,128]{1,0:T(8,128)S(1)}, f32[3272,128]{1,0:T(8,128)S(1)}, u32[]{:S(2)}, u32[]{:S(2)}) collective-permute-start(f32[3272,128]{1,0:T(8,128)S(1)} %shard_map.68), channel_id=1, source_target_pairs={{0,8},{8,0},{16,24},{24,16},{1,9},{9,1},{17,25},{25,17},{2,10},{10... | collective-permute-start | bytes 5025800 | tf_op jit(solution)/shard_map/ppermute | solution.py:414
  82.6 39.5 %collective-permute-start.6 = (f32[3272,128]{1,0:T(8,128)S(1)}, f32[3272,128]{1,0:T(8,128)S(1)}, u32[]{:S(2)}, u32[]{:S(2)}) collective-permute-start(f32[3272,128]{1,0:T(8,128)S(1)} %shard_map.66.token_ref), channel_id=1, source_target_pairs={{0,16},{8,24},{16,0},{24,8},{1,17},{9,25},{17,1},{25,9},{2,18},{10... | collective-permute-start | bytes 5025800 | tf_op jit(solution)/shard_map/ppermute | solution.py:414
  84.3 72.7 %collective-permute-start.4 = (f32[3272,128]{1,0:T(8,128)S(1)}, f32[3272,128]{1,0:T(8,128)S(1)}, u32[]{:S(2)}, u32[]{:S(2)}) collective-permute-start(f32[3272,128]{1,0:T(8,128)S(1)} %shard_map.67.token_ref), channel_id=1, source_target_pairs={{0,24},{8,16},{16,8},{24,0},{1,25},{9,17},{17,9},{25,1},{2,26},{10... | collective-permute-start | bytes 5025800 | tf_op jit(solution)/shard_map/ppermute | solution.py:414
  84.4 87.0 %collective-permute-start.8 = (f32[3272,128]{1,0:T(8,128)S(1)}, f32[3272,128]{1,0:T(8,128)S(1)}, u32[]{:S(2)}, u32[]{:S(2)}) collective-permute-start(f32[3272,128]{1,0:T(8,128)S(1)} %shard_map.65.token_ref), channel_id=1, source_target_pairs={{0,1},{1,0},{2,3},{3,2},{4,5},{5,4},{6,7},{7,6},{8,9},{9,8},{10,11... | collective-permute-start | bytes 5025800 | tf_op jit(solution)/shard_map/ppermute | solution.py:418
  86.1 85.3 %collective-permute-start.10 = (f32[3272,128]{1,0:T(8,128)S(1)}, f32[3272,128]{1,0:T(8,128)S(1)}, u32[]{:S(2)}, u32[]{:S(2)}) collective-permute-start(f32[3272,128]{1,0:T(8,128)S(1)} %collective-permute-done.9), channel_id=1, source_target_pairs={{0,1},{1,0},{2,3},{3,2},{4,5},{5,4},{6,7},{7,6},{8,9},{9,8},{10,11... | collective-permute-start | bytes 5025800 | tf_op jit(solution)/shard_map/ppermute | solution.py:418
  122.0 73.6 %collective-permute-start.7 = (f32[3272,128]{1,0:T(8,128)S(1)}, f32[3272,128]{1,0:T(8,128)S(1)}, u32[]{:S(2)}, u32[]{:S(2)}) collective-permute-start(f32[3272,128]{1,0:T(8,128)S(1)} %collective-permute-done.6), channel_id=1, source_target_pairs={{0,1},{1,0},{2,3},{3,2},{4,5},{5,4},{6,7},{7,6},{8,9},{9,8},{10,11... | collective-permute-start | bytes 5025800 | tf_op jit(solution)/shard_map/ppermute | solution.py:418
  157.0 74.0 %collective-permute-start.5 = (f32[3272,128]{1,0:T(8,128)S(1)}, f32[3272,128]{1,0:T(8,128)S(1)}, u32[]{:S(2)}, u32[]{:S(2)}) collective-permute-start(f32[3272,128]{1,0:T(8,128)S(1)} %collective-permute-done.4), channel_id=1, source_target_pairs={{0,1},{1,0},{2,3},{3,2},{4,5},{5,4},{6,7},{7,6},{8,9},{9,8},{10,11... | collective-permute-start | bytes 5025800 | tf_op jit(solution)/shard_map/ppermute | solution.py:418

commit v2 on v1

v2 whole, which is shorter than its diff:
```python
import functools

import jax
import jax.numpy as jnp
from jax import lax
from jax.experimental import pallas as pl
from jax.experimental.pallas import tpu as pltpu
from jax.sharding import PartitionSpec as P

BS = 64
NNZ = 4
SLOTS = 7
ROW_BLOCKS = 6
MOST_FINE = 3
LANES = 128
PACK = BS * BS // LANES
BEFORE = 1
AFTER = 5
LABEL_ROWS = 8
GROUP = 4
ROW_BITS = 10
FIRST_ROUND = 9

F32 = jnp.float32
BF16 = jnp.bfloat16
ANY = pl.BlockSpec(memory_space=pl.ANY)
HBM = pl.BlockSpec(memory_space=pltpu.HBM)
SMEM = pl.BlockSpec(memory_space=pltpu.SMEM)
VMEM = pl.BlockSpec(memory_space=pltpu.VMEM)


def cost_of(seconds):
    return pl.CostEstimate(flops=int(seconds * 1e15), bytes_accessed=int(seconds * 3e12), transcendentals=0)


SMALL = cost_of(1e-6)


def half_lanes(shape):
    return lax.broadcasted_iota(jnp.int32, shape, 1) < LANES // 2


def turned(value):
    return pltpu.roll(value, LANES // 2, 1)


def split(value):
    high = value.astype(BF16)
    low = (value - high.astype(F32)).astype(BF16)
    return high, low


def factors(packed, natural):
    left = half_lanes((PACK, LANES))
    swapped = turned(packed)
    even = jnp.where(left, packed, swapped)
    odd = jnp.where(left, swapped, packed)
    natural[pl.ds(0, PACK, stride=2), :] = even
    natural[pl.ds(1, PACK, stride=2), :] = odd
    high, low = split(natural[...])
    return even, odd, high, low


def transposed(even, odd, flipped):
    flipped[...] = jnp.concatenate([even, odd, even, odd], axis=0).T[0:BS]
    ordered = jnp.concatenate(
        [flipped[pl.ds(0, PACK, stride=2), :], flipped[pl.ds(1, PACK, stride=2), :]], axis=0
    )
    high, low = split(ordered)
    return jnp.where(half_lanes((BS, LANES)), high.astype(F32), low.astype(F32)).astype(BF16)


def prepare_kernel(fine_rows, q_ref, w_ref, t_ref, natural, flipped):
    @pl.loop(0, fine_rows // 8)
    def _(group):
        for lane in range(8):
            row = group * 8 + lane
            packed = q_ref[pl.ds(group * (8 * PACK) + lane, PACK, stride=8), :]
            even, odd, high, low = factors(packed, natural.at[lane])
            w_ref[row + BEFORE, 0:BS, :] = high
            w_ref[row + BEFORE, BS : 2 * BS, :] = low
            t_ref[row] = transposed(even, odd, flipped.at[lane])


def prepare_edge_kernel(
    fine_rows, before_ref, after_ref, w_in, t_in, w_ref, t_ref, w_edge, t_edge, natural, flipped, sem
):
    for row in range(AFTER + BEFORE):
        source, base = (before_ref, 7) if row == AFTER else (after_ref, row)
        even, odd, high, low = factors(source[pl.ds(base, PACK, stride=8), :], natural.at[row])
        w_edge[row, 0:BS, :] = high
        w_edge[row, BS : 2 * BS, :] = low
        if row < 2:
            t_edge[row] = transposed(even, odd, flipped.at[row])
    copies = [
        pltpu.make_async_copy(w_edge.at[pl.ds(0, AFTER)], w_ref.at[pl.ds(fine_rows + BEFORE, AFTER)], sem.at[0]),
        pltpu.make_async_copy(w_edge.at[pl.ds(AFTER, BEFORE)], w_ref.at[pl.ds(0, BEFORE)], sem.at[1]),
        pltpu.make_async_copy(t_edge, t_ref.at[pl.ds(fine_rows, 2)], sem.at[2]),
    ]
    for copy in copies:
        copy.start()
    for copy in copies:
        copy.wait()


def bucket_kernel(
    shift,
    base,
    capacity,
    fine_rows,
    fine_total,
    home_count,
    rows_of_gx,
    me_ref,
    columns_ref,
    slots_ref,
    aggregate_ref,
    owner_ref,
    edge_ref,
    blocks_ref,
    edge_blocks_ref,
    w_ref,
    t_ref,
    token_ref,
    out_ref,
    used_ref,
    stored,
    fine_list,
    table_list,
    local_list,
    place_of,
    in_sem,
):
    lowest = (me_ref[0] ^ shift) * rows_of_gx
    first_block = me_ref[1] * fine_rows
    flat = lax.broadcasted_iota(jnp.int32, (LABEL_ROWS, LANES), 0) * LANES + lax.broadcasted_iota(
        jnp.int32, (LABEL_ROWS, LANES), 1
    )

    def listing(pair, groups, carry):
        listed, tables, own = carry
        start = pair * 4 + 2
        size = 1 + (groups[1] == groups[0]).astype(jnp.int32) + (groups[2] == groups[0]).astype(jnp.int32)
        owners = [owner_ref[pair * 2], owner_ref[pair * 2 + 1]]
        match = [((owner >= lowest) & (owner < lowest + rows_of_gx)).astype(jnp.int32) for owner in owners]
        local = [lax.rem(owner, home_count) for owner in owners]
        table = [tables, tables + match[0]]
        for step in range(4):
            second = size <= step
            fine_list[listed] = start + step
            table_list[listed] = jnp.where(second, table[1], table[0]) * 8
            local_list[listed] = jnp.where(second, local[1], local[0])
            listed = listed + jnp.where(second, match[1], match[0])
            own = jnp.where(start + step < fine_rows, listed, own)
        return listed, tables + match[0] + match[1], own

    zero = jnp.int32(0)
    last = home_count // 2 - 1
    carry = lax.fori_loop(
        0,
        last,
        lambda pair, carry: listing(pair, [aggregate_ref[pair * 4 + 2 + step] for step in range(3)], carry),
        (zero, zero, zero),
    )
    edge_groups = [aggregate_ref[last * 4 + 2], aggregate_ref[last * 4 + 3], edge_ref[4 * NNZ]]
    listed, tables, own = listing(last, edge_groups, carry)

    def target(index):
        return stored.at[pl.ds(pl.multiple_of(index * 2 * BS, 2 * BS), 2 * BS)]

    @pl.loop(0, own)
    def _(index):
        pltpu.make_async_copy(blocks_ref.at[fine_list[index]], target(index), in_sem).start()

    @pl.loop(own, listed)
    def _(index):
        pltpu.make_async_copy(edge_blocks_ref.at[fine_list[index] - fine_rows], target(index), in_sem).start()

    @pl.loop(0, tables)
    def _(table):
        for slot in range(SLOTS):
            place_of[table * 8 + slot] = -1

    @pl.loop(0, capacity)
    def _(place):
        out_ref[pl.ds(pl.multiple_of(place * PACK, PACK), PACK), :] = jnp.zeros((PACK, LANES), F32)

    groups = (listed + GROUP - 1) // GROUP

    @pl.loop(listed, groups * GROUP)
    def _(index):
        fine_list[index] = 2
        table_list[index] = 0
        local_list[index] = 0

    @pl.loop(0, listed)
    def _(index):
        pltpu.make_async_copy(blocks_ref.at[0], target(0), in_sem).wait()

    left = half_lanes((PACK, LANES))
    left_tall = half_lanes((BS, LANES))

    def main(group, carry):
        used, labels = carry
        results = []
        places = []
        for lane in range(GROUP):
            index = group * GROUP + lane
            real = index < listed
            row = fine_list[index]
            inside = row < fine_rows
            own_row = jnp.where(inside, row, 0)
            edge_row = jnp.where(inside, 0, row - fine_rows)
            products = []
            for k in range(NNZ):
                column = jnp.where(inside, columns_ref[k, own_row], edge_ref[k * 2 + edge_row])
                window = column - first_block + BEFORE
                window = jnp.where(window < 0, window + fine_total, window)
                window = jnp.where(window >= fine_total, window - fine_total, window)
                slot = jnp.where(inside, slots_ref[k, own_row], edge_ref[2 * NNZ + k * 2 + edge_row])
                entry = table_list[index] + slot
                seen = place_of[entry]
                new = (seen < 0) & real
                place = jnp.where(new, used, seen)
                place_of[entry] = place
                used = used + new.astype(jnp.int32)
                valid = real & (place >= base) & (place < base + capacity)
                place = jnp.where(valid, place - base, 0)
                places.append((valid, place))
                label = (slot * 2**ROW_BITS + local_list[index]).astype(F32)
                labels = jnp.where((flat == place) & valid, label, labels)
                packed = stored[pl.ds(index * 2 * BS + k, PACK, stride=NNZ), :]
                high = packed.astype(BF16).astype(F32)
                low = packed - high
                even = jnp.where(left, high, turned(low))
                odd = jnp.where(left, turned(high), low)
                both = jnp.concatenate([even, odd], axis=0).astype(BF16)
                factor = w_ref[window]
                q_high = factor[0:BS]
                q_low = factor[BS : 2 * BS]
                products.append(
                    jnp.dot(
                        jnp.concatenate([both, both], axis=1),
                        jnp.concatenate([q_high, q_high, q_low, q_low], axis=0),
                        preferred_element_type=F32,
                    )
                )
            wide = jnp.concatenate(
                [
                    jnp.where(left_tall, products[0], products[1]),
                    jnp.where(left_tall, products[2], products[3]),
                ],
                axis=1,
            )
            high, low = split(wide)
            factor = t_ref[row]
            results.append(
                jnp.dot(
                    jnp.concatenate([factor, factor], axis=1),
                    jnp.concatenate([high, high, low, low], axis=0),
                    preferred_element_type=F32,
                )
            )
        for lane in range(GROUP):
            for pair in range(2):
                even = results[lane][0:PACK, pair * LANES : (pair + 1) * LANES]
                odd = results[lane][PACK:BS, pair * LANES : (pair + 1) * LANES]
                packed = [jnp.where(left, even, turned(odd)), jnp.where(left, turned(even), odd)]
                for k in range(2):
                    valid, place = places[lane * NNZ + pair * 2 + k]
                    where = pl.ds(pl.multiple_of(place * PACK, PACK), PACK)
                    out_ref[where, :] = out_ref[where, :] + jnp.where(valid, packed[k], 0.0)
        return used, labels

    used, labels = lax.fori_loop(0, groups, main, (zero, jnp.zeros((LABEL_ROWS, LANES), F32)))
    held = jnp.clip(used - base, 0, capacity)
    out_ref[pl.ds(capacity * PACK, LABEL_ROWS), :] = jnp.where(
        flat == LABEL_ROWS * LANES - 1, held.astype(F32), labels
    )
    used_ref[0] = used


def place_kernel(counts, capacity, home_count, clear, me_ref, *refs):
    own_count, partner_count = counts
    sources = refs[: own_count + partner_count]
    out_ref, token_ref, labels, zeros, label_sem, zero_sem, sem = refs[-7:]
    token_ref[0] = 0
    slots, row_groups = out_ref.shape[0], out_ref.shape[1]
    copies = []
    for which, source in enumerate(sources):
        copies.append(
            pltpu.make_async_copy(
                source.at[pl.ds(capacity * PACK, LABEL_ROWS)], labels.at[which], label_sem.at[which]
            )
        )
        copies[-1].start()
    if clear:
        zeros[...] = jnp.zeros_like(zeros)

        @pl.loop(0, slots)
        def _(slot):
            @pl.loop(0, row_groups)
            def _(group):
                pltpu.make_async_copy(zeros, out_ref.at[slot, group], zero_sem).start()

        @pl.loop(0, slots * row_groups)
        def _(step):
            pltpu.make_async_copy(zeros, out_ref.at[0, 0], zero_sem).wait()

    moved = jnp.int32(0)
    for which, source in enumerate(sources):
        copies[which].wait()
        upper = me_ref[2] if which < own_count else 1 - me_ref[2]
        held = labels[which, LABEL_ROWS - 1, 0, LANES - 1].astype(jnp.int32)

        @pl.loop(0, held)
        def _(place):
            label = labels[which, place // LANES, 0, place % LANES].astype(jnp.int32)
            slot = label // 2**ROW_BITS
            row = label % 2**ROW_BITS + upper * home_count
            pltpu.make_async_copy(
                source.at[pl.ds(place * PACK, PACK)], out_ref.at[slot, row // 8, :, row % 8], sem
            ).start()

        moved = moved + held

    @pl.loop(0, moved)
    def _(step):
        pltpu.make_async_copy(sources[0].at[pl.ds(0, PACK)], out_ref.at[0, 0, :, 0], sem).wait()


def placed_into(out, out_type, me, capacity, home_count, token, own, partner):
    sources = [value.reshape(-1, 1, LANES) for value in own + partner]
    clear = out is None
    return pl.pallas_call(
        functools.partial(place_kernel, (len(own), len(partner)), capacity, home_count, clear),
        in_specs=[SMEM] + [ANY] * len(sources) + [ANY if clear else HBM],
        out_specs=[HBM, SMEM],
        out_shape=[out_type, jax.ShapeDtypeStruct((1,), jnp.int32)],
        input_output_aliases={} if clear else {len(sources) + 1: 0},
        scratch_shapes=[
            pltpu.SMEM((len(sources), LABEL_ROWS, 1, LANES), F32),
            pltpu.VMEM((PACK, 8, 1, LANES), F32),
            pltpu.SemaphoreType.DMA((len(sources),)),
            pltpu.SemaphoreType.DMA,
            pltpu.SemaphoreType.DMA,
        ],
        compiler_params=pltpu.CompilerParams(vmem_limit_bytes=32 * 2**20),
        cost_estimate=SMALL,
    )(me, *sources, token if clear else out)


def gate_kernel(value_ref, token_ref, out_ref):
    pass


def gate(value, token):
    return pl.pallas_call(
        gate_kernel,
        in_specs=[ANY, ANY],
        out_specs=ANY,
        out_shape=jax.ShapeDtypeStruct(value.shape, value.dtype),
        input_output_aliases={0: 0},
        cost_estimate=SMALL,
    )(value, token)


def body(blocks, prolong, columns, aggregate, column_slot, owner_row):
    fine_rows = blocks.shape[0]
    home_count = owner_row.shape[0]
    size_gx = lax.axis_size("gx")
    size_gy = lax.axis_size("gy")
    size = size_gx * size_gy
    axes = ("gx", "gy")
    here_gx = lax.axis_index("gx")
    here_gy = lax.axis_index("gy")
    position = lax.axis_index(axes)
    bucket_rows = home_count // size_gx + 1
    most = bucket_rows * ROW_BLOCKS
    capacity = bucket_rows * FIRST_ROUND // 2
    most_fine = -(-bucket_rows * MOST_FINE // GROUP) * GROUP
    me = jnp.stack([here_gx, position, here_gy % 2]).astype(jnp.int32)

    block_view = (
        blocks.reshape(fine_rows, NNZ, PACK, LANES).transpose(0, 2, 1, 3).reshape(fine_rows, NNZ * PACK, LANES)
    )
    q_view = (
        prolong.reshape(fine_rows // 8, 8, PACK, LANES).transpose(0, 2, 1, 3).reshape(fine_rows * PACK, LANES)
    )
    group_rows = 8 * PACK
    backward = [(i, (i - 1) % size) for i in range(size)]
    forward = [(i, (i + 1) % size) for i in range(size)]
    edge_ints = jnp.concatenate(
        [columns.T[:, :2].reshape(-1), column_slot.T[:, :2].reshape(-1), aggregate[:2]]
    )
    edge_ints = lax.ppermute(edge_ints, axes, backward)
    after = lax.ppermute(q_view[:group_rows], axes, backward)
    edge_blocks = lax.ppermute(block_view[:2], axes, backward)
    before = lax.ppermute(q_view[-group_rows:], axes, forward)

    factor_types = [
        jax.ShapeDtypeStruct((fine_rows + BEFORE + AFTER, 2 * BS, LANES), BF16),
        jax.ShapeDtypeStruct((fine_rows + 2, BS, LANES), BF16),
    ]
    right, left = pl.pallas_call(
        functools.partial(prepare_kernel, fine_rows),
        in_specs=[VMEM],
        out_specs=[VMEM] * 2,
        out_shape=factor_types,
        scratch_shapes=[pltpu.VMEM((8, BS, LANES), F32), pltpu.VMEM((8, BS, LANES), F32)],
        compiler_params=pltpu.CompilerParams(vmem_limit_bytes=32 * 2**20),
        cost_estimate=cost_of(5e-6),
    )(q_view)
    right, left = pl.pallas_call(
        functools.partial(prepare_edge_kernel, fine_rows),
        in_specs=[VMEM] * 2 + [ANY] * 2,
        out_specs=[ANY] * 2,
        out_shape=factor_types,
        input_output_aliases={2: 0, 3: 1},
        scratch_shapes=[
            pltpu.VMEM((AFTER + BEFORE, 2 * BS, LANES), BF16),
            pltpu.VMEM((2, BS, LANES), BF16),
            pltpu.VMEM((AFTER + BEFORE, BS, LANES), F32),
            pltpu.VMEM((2, BS, LANES), F32),
            pltpu.SemaphoreType.DMA((3,)),
        ],
        compiler_params=pltpu.CompilerParams(vmem_limit_bytes=32 * 2**20),
        cost_estimate=SMALL,
    )(before, after, right, left)

    def bucket(shift, base, token):
        return pl.pallas_call(
            functools.partial(
                bucket_kernel,
                shift,
                base,
                capacity,
                fine_rows,
                fine_rows * size,
                home_count,
                home_count * size_gy,
            ),
            in_specs=[SMEM] * 6 + [ANY] * 2 + [VMEM] * 2 + [ANY],
            out_specs=[VMEM, SMEM],
            out_shape=[
                jax.ShapeDtypeStruct((capacity * PACK + LABEL_ROWS, LANES), F32),
                jax.ShapeDtypeStruct((1,), jnp.int32),
            ],
            scratch_shapes=[
                pltpu.VMEM((most_fine * 2 * BS, LANES), F32),
                pltpu.SMEM((most_fine + GROUP,), jnp.int32),
                pltpu.SMEM((most_fine + GROUP,), jnp.int32),
                pltpu.SMEM((most_fine + GROUP,), jnp.int32),
                pltpu.SMEM((bucket_rows * 8,), jnp.int32),
                pltpu.SemaphoreType.DMA,
            ],
            compiler_params=pltpu.CompilerParams(vmem_limit_bytes=40 * 2**20),
            cost_estimate=SMALL,
        )(
            me,
            columns.T,
            column_slot.T,
            aggregate,
            owner_row,
            edge_ints,
            block_view,
            edge_blocks,
            right,
            left,
            token,
        )

    def across(value, shift):
        pairs = [(source, source ^ shift) for source in range(size_gx)]
        return lax.ppermute(value, "gx", pairs)

    def partner(value):
        pairs = [(source, source ^ 1) for source in range(size_gy)]
        return lax.ppermute(value, "gy", pairs)

    def across_partner(value, shift):
        pairs = [
            (gx * size_gy + gy, (gx ^ shift) * size_gy + (gy ^ 1)) for gx in range(size_gx) for gy in range(size_gy)
        ]
        return lax.ppermute(value, axes, pairs)

    out_type = pltpu.HBM((SLOTS, 2 * home_count // 8, PACK, 8, 1, LANES), F32)

    def round_of(out, base):
        first = out is None
        own_sent, used = bucket(0, base, me)
        counts = [used]
        from_partner = {0: partner(own_sent)}
        sent = {0: own_sent}
        token = own_sent
        for shift in list(range(2, size_gx)) + [1]:
            sent[shift], used = bucket(shift, base, token)
            counts.append(used)
            token = sent[shift]
        if first:
            token = sent[1] = gate(sent[1], from_partner[0])
        from_partner[1] = across_partner(sent[1], 1)
        arrived = {shift: across(sent[shift], shift) for shift in range(1, size_gx)}
        place = functools.partial(
            placed_into, out_type=out_type, me=me, capacity=capacity, home_count=home_count, token=token
        )
        out, placed = place(out, own=[own_sent], partner=[from_partner[0]])
        for shift in range(2, size_gx):
            value = arrived[shift]
            if first and shift == 3:
                value = gate(value, placed)
            from_partner[shift] = partner(value)
        out, _ = place(out, own=[arrived[1]], partner=[from_partner[1]])
        out, _ = place(out, own=[arrived[2]], partner=[])
        for shift in range(3, size_gx):
            out, _ = place(out, own=[arrived[shift]], partner=[from_partner[shift - 1]])
        out, _ = place(out, own=[], partner=[from_partner[size_gx - 1]])
        return out, counts

    out, counts = round_of(None, 0)
    most_used = lax.pmax(functools.reduce(jnp.maximum, counts)[0], axes)
    for later in range(capacity, most, capacity):
        out = lax.cond(most_used > later, lambda out: round_of(out, later)[0], lambda out: out, out)
    return (
        out.reshape(SLOTS, 2 * home_count // 8, PACK, 8, LANES)
        .transpose(1, 3, 0, 2, 4)
        .reshape(2 * home_count, SLOTS, BS * BS)
    )


def solution(mesh):
    placed = (
        P(("gx", "gy"), None, None),
        P(("gx", "gy"), None),
        P(("gx", "gy"), None),
        P(("gx", "gy")),
        P(("gx", "gy"), None),
        P(("gx", "gy")),
    )
    return jax.shard_map(
        body, mesh=mesh, in_specs=placed, out_specs=P(("gx", "gy"), None, None), check_vma=False
    )
```

time: 235 us -> 233 us (level)
  waiting for transfers between devices: 124 us -> 11.3 us
  blocking collectives: 0 us -> 57.6 us
  Pallas kernels: 89.9 us -> 130 us
  starting transfers between devices: 14.4 us -> 20.7 us
  local copies, waits for them, and re-layouts: 5.08 us -> 9.74 us
  between operations: 0.14 us -> 3.71 us
    ppermute x3, waiting for transfers between devices: 72.2 us -> 0.01 us  [across(): return lax.ppermute(value, 'gx', pairs)]
    pmax x0 -> x1, blocking collectives: none -> 57.6 us  [body(): most_used = lax.pmax(functools.reduce(jnp.maximum, counts)[0], axes)]
    ppermute x4 -> x3, waiting for transfers between devices: 50.5 us -> 0.01 us  [partner(): return lax.ppermute(value, 'gy', pairs)]
    pallas_call x4 -> x5, Pallas kernels: 26.9 us -> 60.3 us  [placed_into(): pl.pallas_call(functools.partial(place_kernel, (len(own), len(partner)),...]
    ppermute x0 -> x1, waiting for transfers between devices: none -> 11.3 us  [across_partner(): return lax.ppermute(value, axes, pairs)]
    pallas_call x4 -> x7, Pallas kernels: 57.9 us -> 62.7 us  [the longest x4 61.1 us: bucket(): pl.pallas_call(functools.partial(bucket_kernel, shift, base, capacity, fi...]
    unnamed x10 -> x36, local copies, waits for them, and re-layouts: 1.61 us -> 6.32 us
    ppermute x4 -> x3, starting transfers between devices: 0.38 us -> 3.82 us  [partner(): return lax.ppermute(value, 'gy', pairs)]
  transfers between devices with their start and end apart: 11 -> 11, of which waited for: 6 -> 1; matrix products, arithmetic and copies ran while one was open for 1% -> 1% of each run, Pallas kernels for 12% -> 44%
where the time goes in v2:
time: 233 us; the launch traced here: 234 us
  Pallas kernels  130 us (56%)
  blocking collectives  57.6 us (25%)
  starting transfers between devices  20.7 us (9%)
  waiting for transfers between devices  11.3 us (5%)
  local copies, waits for them, and re-layouts  9.74 us (4%)
  between operations  3.71 us (2%)
    pallas_call x4, Pallas kernels, bucket(): pl.pallas_call(functools.partial(bucket_kernel, shift, base, capacity, fi...  61.1 us
    pallas_call x5, Pallas kernels, placed_into(): pl.pallas_call(functools.partial(place_kernel, (len(own), len(partner)),...  60.3 us
    pmax x1, blocking collectives, body(): most_used = lax.pmax(functools.reduce(jnp.maximum, counts)[0], axes)  57.6 us
    ppermute x1, waiting for transfers between devices, across_partner(): return lax.ppermute(value, axes, pairs)  11.3 us
    pallas_call x1, Pallas kernels, body(): pl.pallas_call(functools.partial(prepare_kernel, fine_rows), in_specs=[VM...  6.78 us
    ppermute x1, starting transfers between devices, body(): edge_ints = lax.ppermute(edge_ints, axes, backward)  6.37 us
    unnamed x36, local copies, waits for them, and re-layouts  6.32 us
  transfers between devices with their start and end apart: 11, of which 1 were waited for; matrix products, arithmetic and copies ran while one was open for 1% of the time, Pallas kernels for 44%

profile of v2, /device:TPU:0, one launch (start us, length us, event | category | flops | bytes accessed | tf_op | source)
XLA Modules:
  0.0 233.7 jit_solution(1246658321201117868)
XLA Ops:
  0.0 0.8 reshape.75
  0.8 0.8 reshape.76
  1.5 0.7 pad_add_fusion.1
  2.3 6.4 %collective-permute-start.7 = (s32[18]{0:T(128)S(1)}, s32[18]{0:T(128)S(1)}, u32[]{:S(2)}, u32[]{:S(2)}) collective-permute-start(s32[18]{0:T(128)S(1)} %pad_add_fusion.1), channel_id=1, source_target_pairs={{0,31},{1,0},{2,1},{3,2},{4,3},{5,4},{6,5},{7,6},{8,7},{9,8},{10,9... | collective-permute-start | bytes 224 | tf_op jit(solution)/shard_map/ppermute | solution.py:396
  8.6 1.0 slice_bitcast_fusion
  9.6 0.3 collective-permute-start.10
  9.9 1.8 collective-permute-start.9
  11.7 0.9 slice.36
  12.6 3.6 %collective-permute-start.8 = (f32[2,128,128]{2,1,0:T(8,128)S(1)}, f32[2,128,128]{2,1,0:T(8,128)S(1)}, u32[]{:S(2)}, u32[]{:S(2)}) collective-permute-start(f32[2,128,128]{2,1,0:T(8,128)S(1)} %bitcast.98), channel_id=1, source_target_pairs={{0,31},{1,0},{2,1},{3,2},{4,3},{5,4},{6,5},{7,6},{8,7},{9,8},{10,9... | collective-permute-start | bytes 393224 | tf_op jit(solution)/shard_map/ppermute | solution.py:398
  16.2 1.6 copy-done.6
  17.8 6.8 %shard_map.64 = (bf16[134,128,128]{2,1,0:T(8,128)(2,1)}, bf16[130,64,128]{2,1,0:T(8,128)(2,1)S(1)}) custom-call(f32[4096,128]{1,0:T(8,128)S(1)} %bitcast.69), custom_call_target="tpu_custom_call" | custom-call | flops 5000000000 | bytes 15000000 | tf_op jit(solution)/shard_map/pallas_call | solution.py:405
  24.6 0.1 pad_add_fusion.me_ref.token_ref
  24.7 0.0 collective-permute-done.10.after_ref
  24.7 0.0 copy-start.13
  24.7 0.0 copy-start.14
  24.7 0.0 copy-start.15
  24.7 0.0 slice-start
  24.7 0.9 shard_map.65
  25.7 0.0 collective-permute-done.7.edge_ref
  25.7 0.0 collective-permute-done.8.edge_blocks_ref
  25.7 0.0 slice-start.1
  25.8 0.0 slice-start.3
  25.8 16.2 %shard_map.66 = (f32[2440,128]{1,0:T(8,128)S(1)}, s32[1]{0:T(128)}) custom-call(s32[3]{0:T(128)S(1)} %pad_add_fusion.me_ref.token_ref, s32[4,128]{1,0:T(4,128)S(1)} %bitcast.81, s32[4,128]{1,0:T(4,128)S(1)} %bitcast.90, s32[128]{0:T(128)S(1)} %copy-done.14, s32[64]{0:T(128)S(1)} %copy-done.15, s32[18]{0:T(128)S(1)} %collective-permute-done.7.edge_ref, ...), custom_call_target="tpu_custom_call" | custom-call | flops 1000000000 | bytes 3000000 | tf_op jit(solution)/shard_map/pallas_call | solution.py:432
  42.0 0.1 collective-permute-start.12
  42.1 17.0 %shard_map.67 = (f32[2440,128]{1,0:T(8,128)}, s32[1]{0:T(128)}) custom-call(s32[3]{0:T(128)S(1)} %pad_add_fusion.me_ref.token_ref, s32[4,128]{1,0:T(4,128)S(1)} %bitcast.82, s32[4,128]{1,0:T(4,128)S(1)} %bitcast.91, s32[128]{0:T(128)S(1)} %copy-done.14, s32[64]{0:T(128)S(1)} %copy-done.15, s32[18]{0:T(128)S(1)} %collective-permute-done.7.edge_ref, ...), custom_call_target="tpu_custom_call" | custom-call | flops 1000000000 | bytes 3000000 | tf_op jit(solution)/shard_map/pallas_call | solution.py:432
  59.1 0.1 collective-permute-start.14
  59.2 12.6 %shard_map.68 = (f32[2440,128]{1,0:T(8,128)S(1)}, s32[1]{0:T(128)}) custom-call(s32[3]{0:T(128)S(1)} %pad_add_fusion.me_ref.token_ref, s32[4,128]{1,0:T(4,128)S(1)} %bitcast.83, s32[4,128]{1,0:T(4,128)S(1)} %bitcast.92, s32[128]{0:T(128)S(1)} %copy-done.14, s32[64]{0:T(128)S(1)} %copy-done.15, s32[18]{0:T(128)S(1)} %collective-permute-done.7.edge_ref, ...), custom_call_target="tpu_custom_call" | custom-call | flops 1000000000 | bytes 3000000 | tf_op jit(solution)/shard_map/pallas_call | solution.py:432
  71.8 15.3 %shard_map.69 = (f32[2440,128]{1,0:T(8,128)S(1)}, s32[1]{0:T(128)}) custom-call(s32[3]{0:T(128)S(1)} %pad_add_fusion.me_ref.token_ref, s32[4,128]{1,0:T(4,128)S(1)} %bitcast.84, s32[4,128]{1,0:T(4,128)S(1)} %bitcast.93, s32[128]{0:T(128)S(1)} %copy-done.14, s32[64]{0:T(128)S(1)} %copy-done.15, s32[18]{0:T(128)S(1)} %collective-permute-done.7.edge_ref, ...), custom_call_target="tpu_custom_call" | custom-call | flops 1000000000 | bytes 3000000 | tf_op jit(solution)/shard_map/pallas_call | solution.py:432
  87.2 1.0 copy-done.2
  88.2 0.0 collective-permute-done.12.token_ref
  88.2 1.0 copy-done
  89.2 1.1 collective-permute-start.16
  90.3 0.8 collective-permute-start.17
  91.1 3.0 %collective-permute-start.11 = (f32[2440,128]{1,0:T(8,128)}, f32[2440,128]{1,0:T(8,128)S(1)}, u32[]{:S(2)}, u32[]{:S(2)}) collective-permute-start(f32[2440,128]{1,0:T(8,128)} %copy-done.5), channel_id=1, source_target_pairs={{0,24},{8,16},{16,8},{24,0},{1,25},{9,17},{17,9},{25,1},{2,26},{10... | collective-permute-start | bytes 3747848 | tf_op jit(solution)/shard_map/ppermute | solution.py:475
  94.0 0.0 collective-permute-done.14
  94.0 1.6 collective-permute-start.15
  95.7 1.3 copy-done.1
  97.0 1.3 copy-done.3
  98.3 10.5 %shard_map.71 = (f32[7,16,32,8,1,128]{5,4,3,2,1,0:T(1,128)}, s32[1]{0:T(128)}) custom-call(s32[3]{0:T(128)S(1)} %pad_add_fusion.me_ref.token_ref, f32[2440,1,128]{2,1,0:T(1,128)S(1)} %bitcast.55, f32[2440,1,128]{2,1,0:T(1,128)S(1)} %bitcast.54, f32[2440,128]{1,0:T(8,128)S(1)} %copy-done.3), custom_call_target="tpu_custom_call" | custom-call | flops 1000000000 | bytes 3000000 | tf_op jit(solution)/shard_map/pallas_call | solution.py:335
  108.8 0.0 collective-permute-done.16
  108.8 11.3 %collective-permute-done.17 = f32[2440,128]{1,0:T(8,128)S(1)} collective-permute-done((f32[2440,128]{1,0:T(8,128)}, f32[2440,128]{1,0:T(8,128)S(1)}, u32[]{:S(2)}, u32[]{:S(2)}) %collective-permute-start.17) | collective-permute-done | bytes 1249312 | tf_op jit(solution)/shard_map/ppermute | solution.py:485
  120.1 5.9 %shard_map.73 = (f32[7,16,32,8,1,128]{5,4,3,2,1,0:T(1,128)}, s32[1]{0:T(128)}) custom-call(s32[3]{0:T(128)S(1)} %pad_add_fusion.me_ref.token_ref, f32[2440,1,128]{2,1,0:T(1,128)S(1)} %bitcast.63, f32[2440,1,128]{2,1,0:T(1,128)S(1)} %bitcast.64, f32[7,16,32,8,1,128]{5,4,3,2,1,0:T(1,128)} %get-tuple-element.82.refs_2_), custom_call_target="tpu_custom_call", output_to_operand_aliasing={{0}: (3, {})} | custom-call | flops 1000000000 | bytes 3000000 | tf_op jit(solution)/shard_map/pallas_call | solution.py:335
  126.0 33.7 %shard_map.74 = (f32[7,16,32,8,1,128]{5,4,3,2,1,0:T(1,128)}, s32[1]{0:T(128)}) custom-call(s32[3]{0:T(128)S(1)} %pad_add_fusion.me_ref.token_ref, f32[2440,1,128]{2,1,0:T(1,128)} %bitcast.38.refs_0_, f32[7,16,32,8,1,128]{5,4,3,2,1,0:T(1,128)} %get-tuple-element.83.refs_1_), custom_call_target="tpu_custom_call", output_to_operand_aliasing={{0}: (2, {})} | custom-call | flops 1000000000 | bytes 3000000 | tf_op jit(solution)/shard_map/pallas_call | solution.py:335
  159.8 6.1 %shard_map.75 = (f32[7,16,32,8,1,128]{5,4,3,2,1,0:T(1,128)}, s32[1]{0:T(128)}) custom-call(s32[3]{0:T(128)S(1)} %pad_add_fusion.me_ref.token_ref, f32[2440,1,128]{2,1,0:T(1,128)S(1)} %bitcast.57, f32[2440,1,128]{2,1,0:T(1,128)S(1)} %bitcast.61, f32[7,16,32,8,1,128]{5,4,3,2,1,0:T(1,128)} %get-tuple-element.84.refs_2_), custom_call_target="tpu_custom_call", output_to_operand_aliasing={{0}: (3, {})} | custom-call | flops 1000000000 | bytes 3000000 | tf_op jit(solution)/shard_map/pallas_call | solution.py:335
  165.9 0.6 shard_map.72
  166.6 2.1 collective-permute-start.13
  171.3 57.6 %pmax.7 = s32[]{:T(128)} all-reduce(s32[]{:T(128)} %bitcast.31), channel_id=1, replica_groups=mesh['gx'=4,'gy'=8] {'gx','gy'}, use_global_device_ids=true, to_apply=%region_0.1 | all-reduce | flops 1 | bytes 8 | tf_op jit(solution)/shard_map/pmax | solution.py:521
  229.6 4.0 %shard_map.76 = (f32[7,16,32,8,1,128]{5,4,3,2,1,0:T(1,128)}, s32[1]{0:T(128)}) custom-call(s32[3]{0:T(128)S(1)} %pad_add_fusion.me_ref.token_ref, f32[2440,1,128]{2,1,0:T(1,128)S(1)} %bitcast.67, f32[7,16,32,8,1,128]{5,4,3,2,1,0:T(1,128)} %get-tuple-element.85.refs_1_), custom_call_target="tpu_custom_call", output_to_operand_aliasing={{0}: (2, {})} | custom-call | flops 1000000000 | bytes 3000000 | tf_op jit(solution)/shard_map/pallas_call | solution.py:335
  (33 shorter events, 0.1 us)
Async XLA Ops:
  2.3 23.4 %collective-permute-start.7 = (s32[18]{0:T(128)S(1)}, s32[18]{0:T(128)S(1)}, u32[]{:S(2)}, u32[]{:S(2)}) collective-permute-start(s32[18]{0:T(128)S(1)} %pad_add_fusion.1), channel_id=1, source_target_pairs={{0,31},{1,0},{2,1},{3,2},{4,3},{5,4},{6,5},{7,6},{8,7},{9,8},{10,9... | collective-permute-start | bytes 224 | tf_op jit(solution)/shard_map/ppermute | solution.py:396
  9.6 15.0 %collective-permute-start.10 = (f32[256,128]{1,0:T(8,128)S(1)}, f32[256,128]{1,0:T(8,128)S(1)}, u32[]{:S(2)}, u32[]{:S(2)}) collective-permute-start(f32[256,128]{1,0:T(8,128)S(1)} %get-tuple-element.87), channel_id=1, source_target_pairs={{0,31},{1,0},{2,1},{3,2},{4,3},{5,4},{6,5},{7,6},{8,7},{9,8},{10,9... | collective-permute-start | bytes 393224 | tf_op jit(solution)/shard_map/ppermute | solution.py:397
  9.9 14.8 %collective-permute-start.9 = (f32[256,128]{1,0:T(8,128)S(1)}, f32[256,128]{1,0:T(8,128)S(1)}, u32[]{:S(2)}, u32[]{:S(2)}) collective-permute-start(f32[256,128]{1,0:T(8,128)S(1)} %get-tuple-element.88), channel_id=1, source_target_pairs={{0,1},{1,2},{2,3},{3,4},{4,5},{5,6},{6,7},{7,8},{8,9},{9,10},{10,1... | collective-permute-start | bytes 393224 | tf_op jit(solution)/shard_map/ppermute | solution.py:399
  12.6 13.1 %collective-permute-start.8 = (f32[2,128,128]{2,1,0:T(8,128)S(1)}, f32[2,128,128]{2,1,0:T(8,128)S(1)}, u32[]{:S(2)}, u32[]{:S(2)}) collective-permute-start(f32[2,128,128]{2,1,0:T(8,128)S(1)} %bitcast.98), channel_id=1, source_target_pairs={{0,31},{1,0},{2,1},{3,2},{4,3},{5,4},{6,5},{7,6},{8,7},{9,8},{10,9... | collective-permute-start | bytes 393224 | tf_op jit(solution)/shard_map/ppermute | solution.py:398
  16.2 1.6 copy-start.6
  24.7 1.0 copy-start.12
  24.7 1.0 copy-start.13
  24.7 1.0 copy-start.14
  24.7 1.0 copy-start.15
  24.7 17.4 %slice-start = ((s8[8388608]{0:T(1024)(128)(4,1)}), s8[4194304]{0:T(1024)(128)(4,1)S(1)}, s32[]{:S(2)}) async-start(s8[8388608]{0:T(1024)(128)(4,1)} %bitcast.73), calls=%async_computation | async-start | bytes 8388608
  25.7 16.3 %copy-start.9 = (bf16[130,64,128]{2,1,0:T(8,128)(2,1)}, bf16[130,64,128]{2,1,0:T(8,128)(2,1)S(1)}, u32[]{:S(2)}) copy-start(bf16[130,64,128]{2,1,0:T(8,128)(2,1)S(1)} %get-tuple-element.72.t_ref) | copy-start | bytes 6389764
  25.7 16.4 %slice-start.2 = ((s8[4390912]{0:T(1024)(128)(4,1)}), s8[4194304]{0:T(1024)(128)(4,1)S(1)}, s32[]{:S(2)}) async-start(s8[4390912]{0:T(1024)(128)(4,1)} %bitcast.78), calls=%async_computation.2 | async-start | bytes 8388608
  25.7 16.4 %slice-start.1 = ((s8[8388608]{0:T(1024)(128)(4,1)}), s8[4194304]{0:T(1024)(128)(4,1)S(1)}, s32[]{:S(2)}) async-start(s8[8388608]{0:T(1024)(128)(4,1)} %bitcast.73), calls=%async_computation.1 | async-start | bytes 8388608
  25.8 16.4 %slice-start.3 = ((s8[4390912]{0:T(1024)(128)(4,1)}), s8[196608]{0:T(1024)(128)(4,1)S(1)}, s32[]{:S(2)}) async-start(s8[4390912]{0:T(1024)(128)(4,1)} %bitcast.78), calls=%async_computation.3 | async-start | bytes 393216
  42.0 46.2 %collective-permute-start.12 = (f32[2440,128]{1,0:T(8,128)S(1)}, f32[2440,128]{1,0:T(8,128)S(1)}, u32[]{:S(2)}, u32[]{:S(2)}) collective-permute-start(f32[2440,128]{1,0:T(8,128)S(1)} %get-tuple-element.74.token_ref), channel_id=1, source_target_pairs={{0,1},{1,0},{2,3},{3,2},{4,5},{5,4},{6,7},{7,6},{8,9},{9,8},{10,11... | collective-permute-start | bytes 3747848 | tf_op jit(solution)/shard_map/ppermute | solution.py:479
  42.1 17.1 %copy-start.10 = (bf16[130,64,128]{2,1,0:T(8,128)(2,1)S(1)}, bf16[130,64,128]{2,1,0:T(8,128)(2,1)}, u32[]{:S(2)}) copy-start(bf16[130,64,128]{2,1,0:T(8,128)(2,1)} %copy-done.9) | copy-start | bytes 6389764
  59.1 34.9 %collective-permute-start.14 = (f32[2440,128]{1,0:T(8,128)}, f32[2440,128]{1,0:T(8,128)}, u32[]{:S(2)}, u32[]{:S(2)}) collective-permute-start(f32[2440,128]{1,0:T(8,128)} %get-tuple-element.76.token_ref), channel_id=1, source_target_pairs={{0,16},{8,24},{16,0},{24,8},{1,17},{9,25},{17,1},{25,9},{2,18},{10... | collective-permute-start | bytes 3747848 | tf_op jit(solution)/shard_map/ppermute | solution.py:475
  71.8 15.4 %copy-start.5 = (f32[2440,128]{1,0:T(8,128)}, f32[2440,128]{1,0:T(8,128)S(1)}, u32[]{:S(2)}) copy-start(f32[2440,128]{1,0:T(8,128)S(1)} %get-tuple-element.78.token_ref) | copy-start | bytes 3747844
  87.2 1.0 copy-start.2
  88.2 1.0 copy-start
  89.2 19.5 %collective-permute-start.16 = (f32[2440,128]{1,0:T(8,128)}, f32[2440,128]{1,0:T(8,128)S(1)}, u32[]{:S(2)}, u32[]{:S(2)}) collective-permute-start(f32[2440,128]{1,0:T(8,128)} %shard_map.70.refs_2_), channel_id=1, source_target_pairs={{0,8},{8,0},{16,24},{24,16},{1,9},{9,1},{17,25},{25,17},{2,10},{10... | collective-permute-start | bytes 3747848 | tf_op jit(solution)/shard_map/ppermute | solution.py:475
  90.3 29.8 %collective-permute-start.17 = (f32[2440,128]{1,0:T(8,128)}, f32[2440,128]{1,0:T(8,128)S(1)}, u32[]{:S(2)}, u32[]{:S(2)}) collective-permute-start(f32[2440,128]{1,0:T(8,128)} %shard_map.70.refs_2_), channel_id=1, source_target_pairs={{0,9},{1,8},{2,11},{3,10},{4,13},{5,12},{6,15},{7,14},{8,1},{9,0},... | collective-permute-start | bytes 3747848 | tf_op jit(solution)/shard_map/ppermute | solution.py:485
  91.1 68.7 %collective-permute-start.11 = (f32[2440,128]{1,0:T(8,128)}, f32[2440,128]{1,0:T(8,128)S(1)}, u32[]{:S(2)}, u32[]{:S(2)}) collective-permute-start(f32[2440,128]{1,0:T(8,128)} %copy-done.5), channel_id=1, source_target_pairs={{0,24},{8,16},{16,8},{24,0},{1,25},{9,17},{17,9},{25,1},{2,26},{10... | collective-permute-start | bytes 3747848 | tf_op jit(solution)/shard_map/ppermute | solution.py:475
  94.0 65.7 %collective-permute-start.15 = (f32[2440,128]{1,0:T(8,128)}, f32[2440,128]{1,0:T(8,128)S(1)}, u32[]{:S(2)}, u32[]{:S(2)}) collective-permute-start(f32[2440,128]{1,0:T(8,128)} %collective-permute-done.14), channel_id=1, source_target_pairs={{0,1},{1,0},{2,3},{3,2},{4,5},{5,4},{6,7},{7,6},{8,9},{9,8},{10,11... | collective-permute-start | bytes 3747848 | tf_op jit(solution)/shard_map/ppermute | solution.py:479
  95.7 1.3 copy-start.1
  97.0 1.3 copy-start.3
  159.7 6.2 %copy-start.4 = (f32[2440,128]{1,0:T(8,128)}, f32[2440,128]{1,0:T(8,128)S(1)}, u32[]{:S(2)}) copy-start(f32[2440,128]{1,0:T(8,128)S(1)} %collective-permute-done.11.value_ref) | copy-start | bytes 3747844
  166.6 63.0 %collective-permute-start.13 = (f32[2440,128]{1,0:T(8,128)}, f32[2440,128]{1,0:T(8,128)S(1)}, u32[]{:S(2)}, u32[]{:S(2)}) collective-permute-start(f32[2440,128]{1,0:T(8,128)} %shard_map.72), channel_id=1, source_target_pairs={{0,1},{1,0},{2,3},{3,2},{4,5},{5,4},{6,7},{7,6},{8,9},{9,8},{10,11... | collective-permute-start | bytes 3747848 | tf_op jit(solution)/shard_map/ppermute | solution.py:479
  229.6 4.1 %copy-start.11 = (bf16[130,64,128]{2,1,0:T(8,128)(2,1)S(1)}, bf16[130,64,128]{2,1,0:T(8,128)(2,1)}, u32[]{:S(2)}) copy-start(bf16[130,64,128]{2,1,0:T(8,128)(2,1)} %copy-done.9) | copy-start | bytes 6389764

commit v3 on v2

--- a/solution.py
+++ b/solution.py
@@ -50,52 +50,113 @@
     return high, low
 
 
-def factors(packed, natural):
+def halves(packed):
     left = half_lanes((PACK, LANES))
     swapped = turned(packed)
-    even = jnp.where(left, packed, swapped)
-    odd = jnp.where(left, swapped, packed)
+    return jnp.where(left, packed, swapped), jnp.where(left, swapped, packed)
+
+
+def high_and_low(value):
+    high, low = split(value)
+    return jnp.where(half_lanes(value.shape), high.astype(F32), low.astype(F32)).astype(BF16)
+
+
+def factor(packed, natural):
+    even, odd = halves(packed)
     natural[pl.ds(0, PACK, stride=2), :] = even
     natural[pl.ds(1, PACK, stride=2), :] = odd
-    high, low = split(natural[...])
-    return even, odd, high, low
-
-
-def transposed(even, odd, flipped):
+    return high_and_low(natural[...])
+
+
+def transposed(packed, flipped):
+    even, odd = halves(packed)
     flipped[...] = jnp.concatenate([even, odd, even, odd], axis=0).T[0:BS]
-    ordered = jnp.concatenate(
-        [flipped[pl.ds(0, PACK, stride=2), :], flipped[pl.ds(1, PACK, stride=2), :]], axis=0
-    )
-    high, low = split(ordered)
-    return jnp.where(half_lanes((BS, LANES)), high.astype(F32), low.astype(F32)).astype(BF16)
-
-
-def prepare_kernel(fine_rows, q_ref, w_ref, t_ref, natural, flipped):
-    @pl.loop(0, fine_rows // 8)
-    def _(group):
+    return high_and_low(
+        jnp.concatenate([flipped[pl.ds(0, PACK, stride=2), :], flipped[pl.ds(1, PACK, stride=2), :]], axis=0)
+    )
+
+
+def flat_index():
+    shape = (LABEL_ROWS, LANES)
+    return lax.broadcasted_iota(jnp.int32, shape, 0) * LANES + lax.broadcasted_iota(jnp.int32, shape, 1)
+
+
+def edge_kernel(columns_ref, slots_ref, aggregate_ref, q_ref, blocks_ref, back_ref, forth_ref, sem):
+    group_rows = 8 * PACK
+    block_rows = NNZ * PACK
+    copies = [
+        pltpu.make_async_copy(q_ref.at[pl.ds(0, group_rows)], back_ref.at[pl.ds(0, group_rows)], sem.at[0]),
+        pltpu.make_async_copy(
+            q_ref.at[pl.ds(q_ref.shape[0] - group_rows, group_rows)], forth_ref, sem.at[1]
+        ),
+    ]
+    for row in range(2):
+        copies.append(
+            pltpu.make_async_copy(
+                blocks_ref.at[row], back_ref.at[pl.ds(group_rows + row * block_rows, block_rows)], sem.at[2 + row]
+            )
+        )
+    for copy in copies:
+        copy.start()
+    flat = flat_index()
+    values = [ref[k, row] for ref in (columns_ref, slots_ref) for k in range(NNZ) for row in range(2)]
+    numbers = jnp.zeros((LABEL_ROWS, LANES), jnp.int32)
+    for place, value in enumerate(values + [aggregate_ref[0], aggregate_ref[1]]):
+        numbers = jnp.where(flat == place, value, numbers)
+    back_ref[pl.ds(group_rows + 2 * block_rows, LABEL_ROWS), :] = numbers.astype(F32)
+    for copy in copies:
+        copy.wait()
+
+
+def prepare_kernel(
+    fine_rows, rows_of_gx, size_gx, slots_ref, aggregate_ref, owner_ref, q_ref, w_ref, bound_ref, natural
+):
+    def ones(mask):
+        mask = mask - ((mask >> 1) & 0x55)
+        mask = (mask & 0x33) + ((mask >> 2) & 0x33)
+        return (mask + (mask >> 4)) & 0xF
+
+    def blocks_of(pair, counts):
+        rows = [jnp.minimum(pair * 4 + 2 + step, fine_rows - 1) for step in range(4)]
+        masks = []
+        for row in rows:
+            mask = jnp.int32(0)
+            for k in range(NNZ):
+                mask = mask | (jnp.int32(1) << slots_ref[k, row])
+            masks.append(mask)
+        leading = aggregate_ref[rows[0]]
+        second = aggregate_ref[rows[1]] == leading
+        third = aggregate_ref[rows[2]] == leading
+        merged = [
+            masks[0] | jnp.where(second, masks[1], 0) | jnp.where(third, masks[2], 0),
+            masks[3] | jnp.where(second, 0, masks[1]) | jnp.where(third, 0, masks[2]),
+        ]
+        counts = list(counts)
+        for which in range(2):
+            number = jnp.where(pair * 4 + 5 < fine_rows, ones(merged[which]), SLOTS)
+            owner = owner_ref[pair * 2 + which]
+            for gx in range(size_gx):
+                there = (owner >= gx * rows_of_gx) & (owner < (gx + 1) * rows_of_gx)
+                counts[gx] = counts[gx] + jnp.where(there, number, 0)
+        return tuple(counts)
+
+    def eight_rows(group, counts):
         for lane in range(8):
-            row = group * 8 + lane
             packed = q_ref[pl.ds(group * (8 * PACK) + lane, PACK, stride=8), :]
-            even, odd, high, low = factors(packed, natural.at[lane])
-            w_ref[row + BEFORE, 0:BS, :] = high
-            w_ref[row + BEFORE, BS : 2 * BS, :] = low
-            t_ref[row] = transposed(even, odd, flipped.at[lane])
-
-
-def prepare_edge_kernel(
-    fine_rows, before_ref, after_ref, w_in, t_in, w_ref, t_ref, w_edge, t_edge, natural, flipped, sem
-):
+            w_ref[group * 8 + lane + BEFORE] = factor(packed, natural.at[lane])
+        return blocks_of(group * 2 + 1, blocks_of(group * 2, counts))
+
+    counts = lax.fori_loop(0, fine_rows // 8, eight_rows, (jnp.int32(0),) * size_gx)
+    bound_ref[...] = jnp.full(bound_ref.shape, functools.reduce(jnp.maximum, counts).astype(F32))
+
+
+def prepare_edge_kernel(fine_rows, before_ref, edge_ref, w_in, w_ref, w_edge, natural, sem):
     for row in range(AFTER + BEFORE):
-        source, base = (before_ref, 7) if row == AFTER else (after_ref, row)
-        even, odd, high, low = factors(source[pl.ds(base, PACK, stride=8), :], natural.at[row])
-        w_edge[row, 0:BS, :] = high
-        w_edge[row, BS : 2 * BS, :] = low
-        if row < 2:
-            t_edge[row] = transposed(even, odd, flipped.at[row])
+        source, base = (before_ref, 7) if row == AFTER else (edge_ref, row)
+        w_edge[row] = factor(source[pl.ds(base, PACK, stride=8), :], natural.at[row])
     copies = [
         pltpu.make_async_copy(w_edge.at[pl.ds(0, AFTER)], w_ref.at[pl.ds(fine_rows + BEFORE, AFTER)], sem.at[0]),
         pltpu.make_async_copy(w_edge.at[pl.ds(AFTER, BEFORE)], w_ref.at[pl.ds(0, BEFORE)], sem.at[1]),
-        pltpu.make_async_copy(t_edge, t_ref.at[pl.ds(fine_rows, 2)], sem.at[2]),
     ]
     for copy in copies:
         copy.start()
@@ -116,26 +177,34 @@
     slots_ref,
     aggregate_ref,
     owner_ref,
+    blocks_ref,
+    numbers_ref,
     edge_ref,
-    blocks_ref,
-    edge_blocks_ref,
+    q_ref,
     w_ref,
-    t_ref,
     token_ref,
+    other_ref,
     out_ref,
-    used_ref,
     stored,
+    flipped,
+    numbers,
+    edge_list,
     fine_list,
     table_list,
     local_list,
     place_of,
     in_sem,
+    number_sem,
 ):
     lowest = (me_ref[0] ^ shift) * rows_of_gx
     first_block = me_ref[1] * fine_rows
-    flat = lax.broadcasted_iota(jnp.int32, (LABEL_ROWS, LANES), 0) * LANES + lax.broadcasted_iota(
-        jnp.int32, (LABEL_ROWS, LANES), 1
-    )
+    flat = flat_index()
+    block_rows = NNZ * PACK
+    edge_base = 8 * PACK
+    number_copy = pltpu.make_async_copy(
+        numbers_ref.at[pl.ds(edge_base + 2 * block_rows, LABEL_ROWS)], numbers, number_sem
+    )
+    number_copy.start()
 
     def listing(pair, groups, carry):
         listed, tables, own = carry
@@ -162,7 +231,10 @@
         lambda pair, carry: listing(pair, [aggregate_ref[pair * 4 + 2 + step] for step in range(3)], carry),
         (zero, zero, zero),
     )
-    edge_groups = [aggregate_ref[last * 4 + 2], aggregate_ref[last * 4 + 3], edge_ref[4 * NNZ]]
+    number_copy.wait()
+    for place in range(4 * NNZ + 1):
+        edge_list[place] = numbers[0, 0, place].astype(jnp.int32)
+    edge_groups = [aggregate_ref[last * 4 + 2], aggregate_ref[last * 4 + 3], edge_list[4 * NNZ]]
     listed, tables, own = listing(last, edge_groups, carry)
 
     def target(index):
@@ -174,7 +246,9 @@
 
     @pl.loop(own, listed)
     def _(index):
-        pltpu.make_async_copy(edge_blocks_ref.at[fine_list[index] - fine_rows], target(index), in_sem).start()
+        first = edge_base + (fine_list[index] - fine_rows) * block_rows
+        source = edge_ref.at[pl.ds(pl.multiple_of(first, block_rows), block_rows)]
+        pltpu.make_async_copy(source, target(index), in_sem).start()
 
     @pl.loop(0, tables)
     def _(table):
@@ -213,11 +287,11 @@
             edge_row = jnp.where(inside, 0, row - fine_rows)
             products = []
             for k in range(NNZ):
-                column = jnp.where(inside, columns_ref[k, own_row], edge_ref[k * 2 + edge_row])
+                column = jnp.where(inside, columns_ref[k, own_row], edge_list[k * 2 + edge_row])
                 window = column - first_block + BEFORE
                 window = jnp.where(window < 0, window + fine_total, window)
                 window = jnp.where(window >= fine_total, window - fine_total, window)
-                slot = jnp.where(inside, slots_ref[k, own_row], edge_ref[2 * NNZ + k * 2 + edge_row])
+                slot = jnp.where(inside, slots_ref[k, own_row], edge_list[2 * NNZ + k * 2 + edge_row])
                 entry = table_list[index] + slot
                 seen = place_of[entry]
                 new = (seen < 0) & real
@@ -235,16 +309,9 @@
                 even = jnp.where(left, high, turned(low))
                 odd = jnp.where(left, turned(high), low)
                 both = jnp.concatenate([even, odd], axis=0).astype(BF16)
-                factor = w_ref[window]
-                q_high = factor[0:BS]
-                q_low = factor[BS : 2 * BS]
-                products.append(
-                    jnp.dot(
-                        jnp.concatenate([both, both], axis=1),
-                        jnp.concatenate([q_high, q_high, q_low, q_low], axis=0),
-                        preferred_element_type=F32,
-                    )
-                )
+                right = w_ref[window]
+                parts = jnp.dot(both, jnp.concatenate([right, right], axis=0), preferred_element_type=F32)
+                products.append(parts + turned(parts))
             wide = jnp.concatenate(
                 [
                     jnp.where(left_tall, products[0], products[1]),
@@ -253,11 +320,13 @@
                 axis=1,
             )
             high, low = split(wide)
-            factor = t_ref[row]
+            mine = q_ref[pl.ds((own_row // 8) * (8 * PACK) + own_row % 8, PACK, stride=8), :]
+            other = edge_ref[pl.ds(edge_row, PACK, stride=8), :]
+            row = transposed(jnp.where(inside, mine, other), flipped.at[lane])
             results.append(
                 jnp.dot(
-                    jnp.concatenate([factor, factor], axis=1),
-                    jnp.concatenate([high, high, low, low], axis=0),
+                    jnp.concatenate([row, row[:, 0:BS]], axis=1),
+                    jnp.concatenate([high, high, low], axis=0),
                     preferred_element_type=F32,
                 )
             )
@@ -277,7 +346,6 @@
     out_ref[pl.ds(capacity * PACK, LABEL_ROWS), :] = jnp.where(
         flat == LABEL_ROWS * LANES - 1, held.astype(F32), labels
     )
-    used_ref[0] = used
 
 
 def place_kernel(counts, capacity, home_count, clear, me_ref, *refs):
@@ -334,7 +402,7 @@
     clear = out is None
     return pl.pallas_call(
         functools.partial(place_kernel, (len(own), len(partner)), capacity, home_count, clear),
-        in_specs=[SMEM] + [ANY] * len(sources) + [ANY if clear else HBM],
+        in_specs=[SMEM] + [VMEM] * len(sources) + [ANY if clear else HBM],
         out_specs=[HBM, SMEM],
         out_shape=[out_type, jax.ShapeDtypeStruct((1,), jnp.int32)],
         input_output_aliases={} if clear else {len(sources) + 1: 0},
@@ -351,18 +419,22 @@
 
 
 def gate_kernel(value_ref, token_ref, out_ref):
-    pass
+    out_ref[...] = value_ref[...]
 
 
 def gate(value, token):
     return pl.pallas_call(
         gate_kernel,
-        in_specs=[ANY, ANY],
-        out_specs=ANY,
+        in_specs=[VMEM, ANY],
+        out_specs=VMEM,
         out_shape=jax.ShapeDtypeStruct(value.shape, value.dtype),
-        input_output_aliases={0: 0},
+        compiler_params=pltpu.CompilerParams(vmem_limit_bytes=24 * 2**20),
         cost_estimate=SMALL,
     )(value, token)
+
+
+def most_kernel(bounds_ref, token_ref, most_ref):
+    most_ref[0] = jnp.max(bounds_ref[...]).astype(jnp.int32)
 
 
 def body(blocks, prolong, columns, aggregate, column_slot, owner_row):
@@ -387,48 +459,51 @@
     q_view = (
         prolong.reshape(fine_rows // 8, 8, PACK, LANES).transpose(0, 2, 1, 3).reshape(fine_rows * PACK, LANES)
     )
-    group_rows = 8 * PACK
+    edge_rows = 8 * PACK + 2 * NNZ * PACK + LABEL_ROWS
     backward = [(i, (i - 1) % size) for i in range(size)]
     forward = [(i, (i + 1) % size) for i in range(size)]
-    edge_ints = jnp.concatenate(
-        [columns.T[:, :2].reshape(-1), column_slot.T[:, :2].reshape(-1), aggregate[:2]]
-    )
-    edge_ints = lax.ppermute(edge_ints, axes, backward)
-    after = lax.ppermute(q_view[:group_rows], axes, backward)
-    edge_blocks = lax.ppermute(block_view[:2], axes, backward)
-    before = lax.ppermute(q_view[-group_rows:], axes, forward)
-
-    factor_types = [
-        jax.ShapeDtypeStruct((fine_rows + BEFORE + AFTER, 2 * BS, LANES), BF16),
-        jax.ShapeDtypeStruct((fine_rows + 2, BS, LANES), BF16),
-    ]
-    right, left = pl.pallas_call(
-        functools.partial(prepare_kernel, fine_rows),
-        in_specs=[VMEM],
+    back, forth = pl.pallas_call(
+        edge_kernel,
+        in_specs=[SMEM] * 3 + [ANY] * 2,
         out_specs=[VMEM] * 2,
-        out_shape=factor_types,
-        scratch_shapes=[pltpu.VMEM((8, BS, LANES), F32), pltpu.VMEM((8, BS, LANES), F32)],
+        out_shape=[
+            jax.ShapeDtypeStruct((edge_rows, LANES), F32),
+            jax.ShapeDtypeStruct((8 * PACK, LANES), F32),
+        ],
+        scratch_shapes=[pltpu.SemaphoreType.DMA((4,))],
+        compiler_params=pltpu.CompilerParams(vmem_limit_bytes=48 * 2**20),
+        cost_estimate=SMALL,
+    )(columns.T, column_slot.T, aggregate, q_view, block_view)
+    edge = lax.ppermute(back, axes, backward)
+    before = lax.ppermute(forth, axes, forward)
+
+    factor_type = jax.ShapeDtypeStruct((fine_rows + BEFORE + AFTER, BS, LANES), BF16)
+    right, bound = pl.pallas_call(
+        functools.partial(prepare_kernel, fine_rows, home_count * size_gy, size_gx),
+        in_specs=[SMEM] * 3 + [VMEM],
+        out_specs=[VMEM] * 2,
+        out_shape=[factor_type, jax.ShapeDtypeStruct((8, LANES), F32)],
+        scratch_shapes=[pltpu.VMEM((8, BS, LANES), F32)],
         compiler_params=pltpu.CompilerParams(vmem_limit_bytes=32 * 2**20),
         cost_estimate=cost_of(5e-6),
-    )(q_view)
-    right, left = pl.pallas_call(
+    )(column_slot.T, aggregate, owner_row, q_view)
+    bounds = lax.all_gather(bound, axes, tiled=True)
+    right = pl.pallas_call(
         functools.partial(prepare_edge_kernel, fine_rows),
-        in_specs=[VMEM] * 2 + [ANY] * 2,
-        out_specs=[ANY] * 2,
-        out_shape=factor_types,
-        input_output_aliases={2: 0, 3: 1},
+        in_specs=[VMEM] * 2 + [ANY],
+        out_specs=ANY,
+        out_shape=factor_type,
+        input_output_aliases={2: 0},
         scratch_shapes=[
-            pltpu.VMEM((AFTER + BEFORE, 2 * BS, LANES), BF16),
-            pltpu.VMEM((2, BS, LANES), BF16),
+            pltpu.VMEM((AFTER + BEFORE, BS, LANES), BF16),
             pltpu.VMEM((AFTER + BEFORE, BS, LANES), F32),
-            pltpu.VMEM((2, BS, LANES), F32),
-            pltpu.SemaphoreType.DMA((3,)),
+            pltpu.SemaphoreType.DMA((2,)),
         ],
         compiler_params=pltpu.CompilerParams(vmem_limit_bytes=32 * 2**20),
         cost_estimate=SMALL,
-    )(before, after, right, left)
-
-    def bucket(shift, base, token):
+    )(before, edge, right)
+
+    def bucket(shift, base, token, other):
         return pl.pallas_call(
             functools.partial(
                 bucket_kernel,
@@ -440,18 +515,19 @@
                 home_count,
                 home_count * size_gy,
             ),
-            in_specs=[SMEM] * 6 + [ANY] * 2 + [VMEM] * 2 + [ANY],
-            out_specs=[VMEM, SMEM],
-            out_shape=[
-                jax.ShapeDtypeStruct((capacity * PACK + LABEL_ROWS, LANES), F32),
-                jax.ShapeDtypeStruct((1,), jnp.int32),
-            ],
+            in_specs=[SMEM] * 5 + [ANY] * 2 + [VMEM] * 3 + [ANY] * 2,
+            out_specs=VMEM,
+            out_shape=jax.ShapeDtypeStruct((capacity * PACK + LABEL_ROWS, LANES), F32),
             scratch_shapes=[
                 pltpu.VMEM((most_fine * 2 * BS, LANES), F32),
+                pltpu.VMEM((GROUP, BS, LANES), F32),
+                pltpu.SMEM((LABEL_ROWS, 1, LANES), F32),
+                pltpu.SMEM((4 * NNZ + 2,), jnp.int32),
                 pltpu.SMEM((most_fine + GROUP,), jnp.int32),
                 pltpu.SMEM((most_fine + GROUP,), jnp.int32),
                 pltpu.SMEM((most_fine + GROUP,), jnp.int32),
                 pltpu.SMEM((bucket_rows * 8,), jnp.int32),
+                pltpu.SemaphoreType.DMA,
                 pltpu.SemaphoreType.DMA,
             ],
             compiler_params=pltpu.CompilerParams(vmem_limit_bytes=40 * 2**20),
@@ -462,12 +538,13 @@
             column_slot.T,
             aggregate,
             owner_row,
-            edge_ints,
             block_view,
-            edge_blocks,
+            edge.reshape(-1, 1, LANES),
+            edge,
+            q_view,
             right,
-            left,
             token,
+            other,
         )
 
     def across(value, shift):
@@ -488,17 +565,15 @@
 
     def round_of(out, base):
         first = out is None
-        own_sent, used = bucket(0, base, me)
-        counts = [used]
+        own_sent = bucket(0, base, me, me)
         from_partner = {0: partner(own_sent)}
         sent = {0: own_sent}
         token = own_sent
-        for shift in list(range(2, size_gx)) + [1]:
-            sent[shift], used = bucket(shift, base, token)
-            counts.append(used)
+        for shift in [2, 1] + list(range(3, size_gx)):
+            sent[shift] = bucket(shift, base, token, bounds if first and shift == 3 else me)
+            if first and shift == 1:
+                sent[1] = gate(sent[1], from_partner[0])
             token = sent[shift]
-        if first:
-            token = sent[1] = gate(sent[1], from_partner[0])
         from_partner[1] = across_partner(sent[1], 1)
         arrived = {shift: across(sent[shift], shift) for shift in range(1, size_gx)}
         place = functools.partial(
@@ -507,18 +582,24 @@
         out, placed = place(out, own=[own_sent], partner=[from_partner[0]])
         for shift in range(2, size_gx):
             value = arrived[shift]
-            if first and shift == 3:
-                value = gate(value, placed)
+            if first and shift < 4:
+                value = gate(value, from_partner[1] if shift == 2 else placed)
             from_partner[shift] = partner(value)
         out, _ = place(out, own=[arrived[1]], partner=[from_partner[1]])
         out, _ = place(out, own=[arrived[2]], partner=[])
         for shift in range(3, size_gx):
-            out, _ = place(out, own=[arrived[shift]], partner=[from_partner[shift - 1]])
+            out, placed = place(out, own=[arrived[shift]], partner=[from_partner[shift - 1]])
         out, _ = place(out, own=[], partner=[from_partner[size_gx - 1]])
-        return out, counts
-
-    out, counts = round_of(None, 0)
-    most_used = lax.pmax(functools.reduce(jnp.maximum, counts)[0], axes)
+        return out, placed
+
+    out, token = round_of(None, 0)
+    most_used = pl.pallas_call(
+        most_kernel,
+        in_specs=[VMEM, SMEM],
+        out_specs=SMEM,
+        out_shape=jax.ShapeDtypeStruct((1,), jnp.int32),
+        cost_estimate=SMALL,
+    )(bounds, token)[0]
     for later in range(capacity, most, capacity):
         out = lax.cond(most_used > later, lambda out: round_of(out, later)[0], lambda out: out, out)
     return (

time: 233 us -> 237 us (1.017); the launches traced: 234 us -> 235 us
  blocking collectives: 57.6 us -> 86 us
  Pallas kernels: 130 us -> 104 us
  waiting for transfers between devices: 11.3 us -> 32.7 us
  starting transfers between devices: 20.7 us -> 9.89 us
  local copies, waits for them, and re-layouts: 9.74 us -> 2.13 us
  between operations: 3.71 us -> 0.89 us
    all_gather x0 -> x1, blocking collectives: none -> 86 us  [body(): bounds = lax.all_gather(bound, axes, tiled=True)]
    pmax x1 -> x0, blocking collectives: 57.6 us -> none  [body(): most_used = lax.pmax(functools.reduce(jnp.maximum, counts)[0], axes)]
    pallas_call x5, Pallas kernels: 60.3 us -> 30.4 us  [placed_into(): pl.pallas_call(functools.partial(place_kernel, (len(own), len(partner)),...]
    ppermute x3, waiting for transfers between devices: 0.01 us -> 17 us  [across(): return lax.ppermute(value, 'gx', pairs)]
    ppermute x1, waiting for transfers between devices: 11.3 us -> 0.01 us  [across_partner(): return lax.ppermute(value, axes, pairs)]
    ppermute x3, waiting for transfers between devices: 0.01 us -> 9.24 us  [partner(): return lax.ppermute(value, 'gy', pairs)]
    ppermute x4 -> x2, waiting for transfers between devices: 0.01 us -> 6.44 us  [the longest x1 6.43 us: body(): before = lax.ppermute(forth, axes, forward)]
    ppermute x4 -> x2, starting transfers between devices: 12 us -> 6.44 us  [the longest x1 6.44 us: body(): edge = lax.ppermute(back, axes, backward)]
  transfers between devices with their start and end apart: 11 -> 9, of which waited for: 1 -> 3; matrix products, arithmetic and copies ran while one was open for 1% -> 0% of each run, Pallas kernels for 44% -> 35%
where the time goes in v3:
time: 237 us; the launch traced here: 235 us
  Pallas kernels  104 us (44%)
  blocking collectives  86 us (36%)
  waiting for transfers between devices  32.7 us (14%)
  starting transfers between devices  9.89 us (4%)
    all_gather x1, blocking collectives, body(): bounds = lax.all_gather(bound, axes, tiled=True)  86 us
    pallas_call x4, Pallas kernels, bucket(): pl.pallas_call(functools.partial(bucket_kernel, shift, base, capacity, fi...  65.1 us
    pallas_call x5, Pallas kernels, placed_into(): pl.pallas_call(functools.partial(place_kernel, (len(own), len(partner)),...  30.4 us
    ppermute x3, waiting for transfers between devices, across(): return lax.ppermute(value, 'gx', pairs)  17 us
    ppermute x3, waiting for transfers between devices, partner(): return lax.ppermute(value, 'gy', pairs)  9.24 us
    ppermute x1, starting transfers between devices, body(): edge = lax.ppermute(back, axes, backward)  6.44 us
    ppermute x1, waiting for transfers between devices, body(): before = lax.ppermute(forth, axes, forward)  6.43 us
  transfers between devices with their start and end apart: 9, of which 3 were waited for; matrix products, arithmetic and copies ran while one was open for 0% of the time, Pallas kernels for 35%

profile of v3, /device:TPU:0, one launch (start us, length us, event | category | flops | bytes accessed | tf_op | source)
XLA Modules:
  0.0 235.3 jit_solution(12031178728118765839)
XLA Ops:
  0.0 1.9 shard_map.65
  1.9 6.4 %collective-permute-start.7 = (f32[520,128]{1,0:T(8,128)S(1)}, f32[520,128]{1,0:T(8,128)S(1)}, u32[]{:S(2)}, u32[]{:S(2)}) collective-permute-start(f32[520,128]{1,0:T(8,128)S(1)} %get-tuple-element.56), channel_id=1, source_target_pairs={{0,31},{1,0},{2,1},{3,2},{4,3},{5,4},{6,5},{7,6},{8,7},{9,8},{10,9... | collective-permute-start | bytes 798728 | tf_op jit(solution)/shard_map/ppermute | solution.py:477
  8.3 0.0 collective-permute-start.8
  8.4 0.0 copy-done.4
  8.4 0.0 copy-done.7
  8.4 0.0 copy-done.9
  8.4 0.0 copy-done.10
  8.4 0.0 copy-start.8
  8.4 2.8 %shard_map.64 = (bf16[134,64,128]{2,1,0:T(8,128)(2,1)S(1)}, f32[8,128]{1,0:T(8,128)S(1)}) custom-call(s32[4,128]{1,0:T(4,128)S(1)} %bitcast.89, s32[128]{0:T(128)S(1)} %copy-done.9, s32[64]{0:T(128)S(1)} %copy-done.10, f32[4096,128]{1,0:T(8,128)S(1)} %bitcast.74), custom_call_target="tpu_custom_call" | custom-call | flops 5000000000 | bytes 15000000 | tf_op jit(solution)/shard_map/pallas_call | solution.py:481
  11.2 0.1 pad_add_fusion.me_ref.token_ref.other_ref
  11.3 6.4 %collective-permute-done.8.before_ref = f32[256,128]{1,0:T(8,128)S(1)} collective-permute-done((f32[256,128]{1,0:T(8,128)S(1)}, f32[256,128]{1,0:T(8,128)S(1)}, u32[]{:S(2)}, u32[]{:S(2)}) %collective-permute-start.8) | collective-permute-done | bytes 131104 | tf_op jit(solution)/shard_map/ppermute | solution.py:478
  17.7 0.0 collective-permute-done.7.edge_ref
  17.7 0.3 shard_map.66.w_ref
  18.0 0.0 copy-start.2
  18.0 0.0 copy-done.8
  18.0 2.1 copy-done.5
  20.1 13.9 %shard_map.67.token_ref = f32[2440,128]{1,0:T(8,128)S(1)} custom-call(s32[3]{0:T(128)S(1)} %pad_add_fusion.me_ref.token_ref.other_ref, s32[4,128]{1,0:T(4,128)S(1)} %bitcast.99, s32[4,128]{1,0:T(4,128)S(1)} %bitcast.90, s32[128]{0:T(128)S(1)} %copy-done.9, s32[64]{0:T(128)S(1)} %copy-done.10, f32[128,128,128]{2,1,0:T(8,128)} %bitcast.66, ...), custom_call_target="tpu_custom_call" | custom-call | flops 1000000000 | bytes 3000000 | tf_op jit(solution)/shard_map/pallas_call | solution.py:507
  34.0 0.1 collective-permute-start.9
  34.1 0.0 slice-done
  34.1 0.0 slice-done.1
  34.1 15.8 %shard_map.68.token_ref = f32[2440,128]{1,0:T(8,128)S(1)} custom-call(s32[3]{0:T(128)S(1)} %pad_add_fusion.me_ref.token_ref.other_ref, s32[4,128]{1,0:T(4,128)S(1)} %bitcast.100, s32[4,128]{1,0:T(4,128)S(1)} %bitcast.91, s32[128]{0:T(128)S(1)} %copy-done.9, s32[64]{0:T(128)S(1)} %copy-done.10, f32[128,128,128]{2,1,0:T(8,128)S(1)} %bitcast.70, ...), custom_call_target="tpu_custom_call" | custom-call | flops 1000000000 | bytes 3000000 | tf_op jit(solution)/shard_map/pallas_call | solution.py:507
  50.0 2.5 %collective-permute-start.11 = (f32[2440,128]{1,0:T(8,128)S(1)}, f32[2440,128]{1,0:T(8,128)S(1)}, u32[]{:S(2)}, u32[]{:S(2)}) collective-permute-start(f32[2440,128]{1,0:T(8,128)S(1)} %shard_map.68.token_ref), channel_id=1, source_target_pairs={{0,16},{8,24},{16,0},{24,8},{1,17},{9,25},{17,1},{25,9},{2,18},{10... | collective-permute-start | bytes 3747848 | tf_op jit(solution)/shard_map/ppermute | solution.py:552
  52.4 19.3 %shard_map.69.value_ref = f32[2440,128]{1,0:T(8,128)S(1)} custom-call(s32[3]{0:T(128)S(1)} %pad_add_fusion.me_ref.token_ref.other_ref, s32[4,128]{1,0:T(4,128)S(1)} %bitcast.101, s32[4,128]{1,0:T(4,128)S(1)} %bitcast.92, s32[128]{0:T(128)S(1)} %copy-done.9, s32[64]{0:T(128)S(1)} %copy-done.10, f32[128,128,128]{2,1,0:T(8,128)S(1)} %bitcast.71, ...), custom_call_target="tpu_custom_call" | custom-call | flops 1000000000 | bytes 3000000 | tf_op jit(solution)/shard_map/pallas_call | solution.py:507
  71.8 0.0 collective-permute-done.9.token_ref
  71.8 0.1 shard_map.70.token_ref
  71.9 0.1 collective-permute-start.12
  72.0 86.0 %all_gather.3.other_ref.bounds_ref = f32[256,128]{1,0:T(8,128)S(1)} all-gather(f32[8,128]{1,0:T(8,128)S(1)} %get-tuple-element.55), channel_id=1, replica_groups=mesh['gx'=4,'gy'=8] {'gx','gy'}, dimensions={0}, use_global_device_ids=true | all-gather | bytes 135168 | tf_op jit(solution)/shard_map/all_gather | solution.py:490
  158.0 0.0 copy-done.2
  158.0 16.0 %shard_map.71.refs_2_ = f32[2440,128]{1,0:T(8,128)S(1)} custom-call(s32[3]{0:T(128)S(1)} %pad_add_fusion.me_ref.token_ref.other_ref, s32[4,128]{1,0:T(4,128)S(1)} %bitcast.102, s32[4,128]{1,0:T(4,128)S(1)} %bitcast.93, s32[128]{0:T(128)S(1)} %copy-done.9, s32[64]{0:T(128)S(1)} %copy-done.10, f32[128,128,128]{2,1,0:T(8,128)S(1)} %bitcast.72, ...), custom_call_target="tpu_custom_call" | custom-call | flops 1000000000 | bytes 3000000 | tf_op jit(solution)/shard_map/pallas_call | solution.py:507
  174.0 0.0 copy-done
  174.0 0.1 collective-permute-start.10
  174.1 0.1 collective-permute-start.14
  174.2 0.0 collective-permute-done.11.value_ref
  174.2 0.0 collective-permute-done.12.token_ref
  174.2 0.1 shard_map.72
  174.3 0.1 collective-permute-start.13
  174.4 10.1 %shard_map.73 = (f32[7,16,32,8,1,128]{5,4,3,2,1,0:T(1,128)}, s32[1]{0:T(128)}) custom-call(s32[3]{0:T(128)S(1)} %pad_add_fusion.me_ref.token_ref.other_ref, f32[2440,1,128]{2,1,0:T(1,128)S(1)} %bitcast.50, f32[2440,1,128]{2,1,0:T(1,128)S(1)} %bitcast.52, f32[2440,128]{1,0:T(8,128)S(1)} %shard_map.71.refs_2_), custom_call_target="tpu_custom_call" | custom-call | flops 1000000000 | bytes 3000000 | tf_op jit(solution)/shard_map/pallas_call | solution.py:403
  184.5 17.0 %collective-permute-done.10.value_ref = f32[2440,128]{1,0:T(8,128)S(1)} collective-permute-done((f32[2440,128]{1,0:T(8,128)S(1)}, f32[2440,128]{1,0:T(8,128)S(1)}, u32[]{:S(2)}, u32[]{:S(2)}) %collective-permute-start.10) | collective-permute-done | bytes 1249312 | tf_op jit(solution)/shard_map/ppermute | solution.py:552
  201.6 0.8 shard_map.78
  202.3 0.6 collective-permute-start.15
  203.0 0.0 collective-permute-done.14
  203.0 5.9 %shard_map.74 = (f32[7,16,32,8,1,128]{5,4,3,2,1,0:T(1,128)}, s32[1]{0:T(128)}) custom-call(s32[3]{0:T(128)S(1)} %pad_add_fusion.me_ref.token_ref.other_ref, f32[2440,1,128]{2,1,0:T(1,128)S(1)} %bitcast.60, f32[2440,1,128]{2,1,0:T(1,128)S(1)} %bitcast.51, f32[7,16,32,8,1,128]{5,4,3,2,1,0:T(1,128)} %get-tuple-element.59.refs_2_), custom_call_target="tpu_custom_call", output_to_operand_aliasing={{0}: (3, {})} | custom-call | flops 1000000000 | bytes 3000000 | tf_op jit(solution)/shard_map/pallas_call | solution.py:403
  208.8 4.0 %shard_map.75 = (f32[7,16,32,8,1,128]{5,4,3,2,1,0:T(1,128)}, s32[1]{0:T(128)}) custom-call(s32[3]{0:T(128)S(1)} %pad_add_fusion.me_ref.token_ref.other_ref, f32[2440,1,128]{2,1,0:T(1,128)S(1)} %bitcast.53, f32[7,16,32,8,1,128]{5,4,3,2,1,0:T(1,128)} %get-tuple-element.60.refs_1_), custom_call_target="tpu_custom_call", output_to_operand_aliasing={{0}: (2, {})} | custom-call | flops 1000000000 | bytes 3000000 | tf_op jit(solution)/shard_map/pallas_call | solution.py:403
  212.9 0.0 collective-permute-done.13
  212.9 6.1 %shard_map.76 = (f32[7,16,32,8,1,128]{5,4,3,2,1,0:T(1,128)}, s32[1]{0:T(128)}) custom-call(s32[3]{0:T(128)S(1)} %pad_add_fusion.me_ref.token_ref.other_ref, f32[2440,1,128]{2,1,0:T(1,128)S(1)} %bitcast.55, f32[2440,1,128]{2,1,0:T(1,128)S(1)} %bitcast.57, f32[7,16,32,8,1,128]{5,4,3,2,1,0:T(1,128)} %get-tuple-element.61.refs_2_), custom_call_target="tpu_custom_call", output_to_operand_aliasing={{0}: (3, {})} | custom-call | flops 1000000000 | bytes 3000000 | tf_op jit(solution)/shard_map/pallas_call | solution.py:403
  218.9 2.2 shard_map.77
  221.8 9.2 %collective-permute-done.15 = f32[2440,128]{1,0:T(8,128)S(1)} collective-permute-done((f32[2440,128]{1,0:T(8,128)S(1)}, f32[2440,128]{1,0:T(8,128)S(1)}, u32[]{:S(2)}, u32[]{:S(2)}) %collective-permute-start.15) | collective-permute-done | bytes 1249312 | tf_op jit(solution)/shard_map/ppermute | solution.py:556
  231.0 4.3 %shard_map.79 = (f32[7,16,32,8,1,128]{5,4,3,2,1,0:T(1,128)}, s32[1]{0:T(128)}) custom-call(s32[3]{0:T(128)S(1)} %pad_add_fusion.me_ref.token_ref.other_ref, f32[2440,1,128]{2,1,0:T(1,128)S(1)} %bitcast.64, f32[7,16,32,8,1,128]{5,4,3,2,1,0:T(1,128)} %get-tuple-element.64.refs_1_), custom_call_target="tpu_custom_call", output_to_operand_aliasing={{0}: (2, {})} | custom-call | flops 1000000000 | bytes 3000000 | tf_op jit(solution)/shard_map/pallas_call | solution.py:403
  (14 shorter events, 0.0 us)
Async XLA Ops:
  0.0 8.4 %copy-start.4 = (f32[128,4096]{1,0:T(8,128)S(1)}, f32[128,4096]{1,0:T(8,128)}, u32[]{:S(2)}) copy-start(f32[128,4096]{1,0:T(8,128)} %param.9) | copy-start | bytes 6291460
  0.0 8.4 %copy-start.7 = (s32[128,4]{0,1:T(4,128)S(1)}, s32[128,4]{0,1:T(4,128)}, u32[]{:S(2)}) copy-start(s32[128,4]{0,1:T(4,128)} %param.12) | copy-start | bytes 6148
  0.0 8.4 %copy-start.9 = (s32[128]{0:T(128)S(1)}, s32[128]{0:T(128)}, u32[]{:S(2)}) copy-start(s32[128]{0:T(128)} %aggregate_ref.11) | copy-start | bytes 1540
  0.0 8.4 %copy-start.10 = (s32[64]{0:T(128)S(1)}, s32[64]{0:T(128)}, u32[]{:S(2)}) copy-start(s32[64]{0:T(128)} %owner_ref.9) | copy-start | bytes 772
  1.9 15.8 %collective-permute-start.7 = (f32[520,128]{1,0:T(8,128)S(1)}, f32[520,128]{1,0:T(8,128)S(1)}, u32[]{:S(2)}, u32[]{:S(2)}) collective-permute-start(f32[520,128]{1,0:T(8,128)S(1)} %get-tuple-element.56), channel_id=1, source_target_pairs={{0,31},{1,0},{2,1},{3,2},{4,3},{5,4},{6,5},{7,6},{8,7},{9,8},{10,9... | collective-permute-start | bytes 798728 | tf_op jit(solution)/shard_map/ppermute | solution.py:477
  8.3 9.3 %collective-permute-start.8 = (f32[256,128]{1,0:T(8,128)S(1)}, f32[256,128]{1,0:T(8,128)S(1)}, u32[]{:S(2)}, u32[]{:S(2)}) collective-permute-start(f32[256,128]{1,0:T(8,128)S(1)} %get-tuple-element.57), channel_id=1, source_target_pairs={{0,1},{1,2},{2,3},{3,4},{4,5},{5,6},{6,7},{7,8},{8,9},{9,10},{10,1... | collective-permute-start | bytes 393224 | tf_op jit(solution)/shard_map/ppermute | solution.py:478
  8.4 9.6 %copy-start.8 = (s32[128,4]{0,1:T(4,128)S(1)}, s32[128,4]{0,1:T(4,128)}, u32[]{:S(2)}) copy-start(s32[128,4]{0,1:T(4,128)} %param.10) | copy-start | bytes 6148
  17.7 2.4 %copy-start.5 = (f32[128,4096]{1,0:T(8,128)S(1)}, f32[128,4096]{1,0:T(8,128)}, u32[]{:S(2)}) copy-start(f32[128,4096]{1,0:T(8,128)} %param.9) | copy-start | bytes 6291460
  17.7 16.4 %slice-start = ((s8[8388608]{0:T(1024)(128)(4,1)}), s8[4194304]{0:T(1024)(128)(4,1)S(1)}, s32[]{:S(2)}) async-start(s8[8388608]{0:T(1024)(128)(4,1)} %bitcast.68), calls=%async_computation | async-start | bytes 8388608
  18.0 140.0 %copy-start.2 = (bf16[134,64,128]{2,1,0:T(8,128)(2,1)}, bf16[134,64,128]{2,1,0:T(8,128)(2,1)S(1)}, u32[]{:S(2)}) copy-start(bf16[134,64,128]{2,1,0:T(8,128)(2,1)S(1)} %shard_map.66.w_ref) | copy-start | bytes 6586372
  20.1 14.0 %slice-start.1 = ((s8[8388608]{0:T(1024)(128)(4,1)}), s8[4194304]{0:T(1024)(128)(4,1)S(1)}, s32[]{:S(2)}) async-start(s8[8388608]{0:T(1024)(128)(4,1)} %bitcast.68), calls=%async_computation.1 | async-start | bytes 8388608
  34.0 37.8 %collective-permute-start.9 = (f32[2440,128]{1,0:T(8,128)S(1)}, f32[2440,128]{1,0:T(8,128)S(1)}, u32[]{:S(2)}, u32[]{:S(2)}) collective-permute-start(f32[2440,128]{1,0:T(8,128)S(1)} %shard_map.67.token_ref), channel_id=1, source_target_pairs={{0,1},{1,0},{2,3},{3,2},{4,5},{5,4},{6,7},{7,6},{8,9},{9,8},{10,11... | collective-permute-start | bytes 3747848 | tf_op jit(solution)/shard_map/ppermute | solution.py:556
  50.0 124.2 %collective-permute-start.11 = (f32[2440,128]{1,0:T(8,128)S(1)}, f32[2440,128]{1,0:T(8,128)S(1)}, u32[]{:S(2)}, u32[]{:S(2)}) collective-permute-start(f32[2440,128]{1,0:T(8,128)S(1)} %shard_map.68.token_ref), channel_id=1, source_target_pairs={{0,16},{8,24},{16,0},{24,8},{1,17},{9,25},{17,1},{25,9},{2,18},{10... | collective-permute-start | bytes 3747848 | tf_op jit(solution)/shard_map/ppermute | solution.py:552
  71.9 102.3 %collective-permute-start.12 = (f32[2440,128]{1,0:T(8,128)S(1)}, f32[2440,128]{1,0:T(8,128)S(1)}, u32[]{:S(2)}, u32[]{:S(2)}) collective-permute-start(f32[2440,128]{1,0:T(8,128)S(1)} %shard_map.70.token_ref), channel_id=1, source_target_pairs={{0,9},{1,8},{2,11},{3,10},{4,13},{5,12},{6,15},{7,14},{8,1},{9,0},... | collective-permute-start | bytes 3747848 | tf_op jit(solution)/shard_map/ppermute | solution.py:562
  158.0 16.0 %copy-start = (f32[256,128]{1,0:T(8,128)}, f32[256,128]{1,0:T(8,128)S(1)}, u32[]{:S(2)}) copy-start(f32[256,128]{1,0:T(8,128)S(1)} %all_gather.3.other_ref.bounds_ref) | copy-start | bytes 393220
  174.0 27.5 %collective-permute-start.10 = (f32[2440,128]{1,0:T(8,128)S(1)}, f32[2440,128]{1,0:T(8,128)S(1)}, u32[]{:S(2)}, u32[]{:S(2)}) collective-permute-start(f32[2440,128]{1,0:T(8,128)S(1)} %shard_map.71.refs_2_), channel_id=1, source_target_pairs={{0,24},{8,16},{16,8},{24,0},{1,25},{9,17},{17,9},{25,1},{2,26},{10... | collective-permute-start | bytes 3747848 | tf_op jit(solution)/shard_map/ppermute | solution.py:552
  174.1 28.8 %collective-permute-start.14 = (f32[2440,128]{1,0:T(8,128)S(1)}, f32[2440,128]{1,0:T(8,128)S(1)}, u32[]{:S(2)}, u32[]{:S(2)}) collective-permute-start(f32[2440,128]{1,0:T(8,128)S(1)} %shard_map.70.token_ref), channel_id=1, source_target_pairs={{0,8},{8,0},{16,24},{24,16},{1,9},{9,1},{17,25},{25,17},{2,10},{10... | collective-permute-start | bytes 3747848 | tf_op jit(solution)/shard_map/ppermute | solution.py:552
  174.3 38.5 %collective-permute-start.13 = (f32[2440,128]{1,0:T(8,128)S(1)}, f32[2440,128]{1,0:T(8,128)S(1)}, u32[]{:S(2)}, u32[]{:S(2)}) collective-permute-start(f32[2440,128]{1,0:T(8,128)S(1)} %shard_map.72), channel_id=1, source_target_pairs={{0,1},{1,0},{2,3},{3,2},{4,5},{5,4},{6,7},{7,6},{8,9},{9,8},{10,11... | collective-permute-start | bytes 3747848 | tf_op jit(solution)/shard_map/ppermute | solution.py:556
  202.3 28.6 %collective-permute-start.15 = (f32[2440,128]{1,0:T(8,128)S(1)}, f32[2440,128]{1,0:T(8,128)S(1)}, u32[]{:S(2)}, u32[]{:S(2)}) collective-permute-start(f32[2440,128]{1,0:T(8,128)S(1)} %shard_map.78), channel_id=1, source_target_pairs={{0,1},{1,0},{2,3},{3,2},{4,5},{5,4},{6,7},{7,6},{8,9},{9,8},{10,11... | collective-permute-start | bytes 3747848 | tf_op jit(solution)/shard_map/ppermute | solution.py:556
  231.0 4.3 %copy-start.3 = (bf16[134,64,128]{2,1,0:T(8,128)(2,1)S(1)}, bf16[134,64,128]{2,1,0:T(8,128)(2,1)}, u32[]{:S(2)}) copy-start(bf16[134,64,128]{2,1,0:T(8,128)(2,1)} %copy-done.2) | copy-start | bytes 6586372
  231.0 4.3 %copy-start.6 = (f32[128,4096]{1,0:T(8,128)S(1)}, f32[128,4096]{1,0:T(8,128)}, u32[]{:S(2)}) copy-start(f32[128,4096]{1,0:T(8,128)} %param.9) | copy-start | bytes 6291460

commit v4 on v3

--- a/solution.py
+++ b/solution.py
@@ -418,19 +418,19 @@
     )(me, *sources, token if clear else out)
 
 
-def gate_kernel(value_ref, token_ref, out_ref):
+def gate_kernel(value_ref, token_ref, other_ref, out_ref):
     out_ref[...] = value_ref[...]
 
 
-def gate(value, token):
+def gate(value, token, other):
     return pl.pallas_call(
         gate_kernel,
-        in_specs=[VMEM, ANY],
+        in_specs=[VMEM, ANY, ANY],
         out_specs=VMEM,
         out_shape=jax.ShapeDtypeStruct(value.shape, value.dtype),
         compiler_params=pltpu.CompilerParams(vmem_limit_bytes=24 * 2**20),
         cost_estimate=SMALL,
-    )(value, token)
+    )(value, token, other)
 
 
 def most_kernel(bounds_ref, token_ref, most_ref):
@@ -487,7 +487,6 @@
         compiler_params=pltpu.CompilerParams(vmem_limit_bytes=32 * 2**20),
         cost_estimate=cost_of(5e-6),
     )(column_slot.T, aggregate, owner_row, q_view)
-    bounds = lax.all_gather(bound, axes, tiled=True)
     right = pl.pallas_call(
         functools.partial(prepare_edge_kernel, fine_rows),
         in_specs=[VMEM] * 2 + [ANY],
@@ -561,6 +560,12 @@
         ]
         return lax.ppermute(value, axes, pairs)
 
+    bits = [1 << bit for bit in range(size.bit_length() - 1)]
+
+    def agreed_with(value, step):
+        pairs = [(source, source ^ step) for source in range(size)]
+        return jnp.maximum(value, lax.ppermute(value, axes, pairs))
+
     out_type = pltpu.HBM((SLOTS, 2 * home_count // 8, PACK, 8, 1, LANES), F32)
 
     def round_of(out, base):
@@ -570,9 +575,9 @@
         sent = {0: own_sent}
         token = own_sent
         for shift in [2, 1] + list(range(3, size_gx)):
-            sent[shift] = bucket(shift, base, token, bounds if first and shift == 3 else me)
+            sent[shift] = bucket(shift, base, token, me)
             if first and shift == 1:
-                sent[1] = gate(sent[1], from_partner[0])
+                sent[1] = gate(sent[1], from_partner[0], me)
             token = sent[shift]
         from_partner[1] = across_partner(sent[1], 1)
         arrived = {shift: across(sent[shift], shift) for shift in range(1, size_gx)}
@@ -582,26 +587,33 @@
         out, placed = place(out, own=[own_sent], partner=[from_partner[0]])
         for shift in range(2, size_gx):
             value = arrived[shift]
-            if first and shift < 4:
-                value = gate(value, from_partner[1] if shift == 2 else placed)
+            if first and shift == 2:
+                agreed = bound
+                for step in [bit for bit in bits if 1 < bit < 2 * size_gy] + [1]:
+                    agreed = agreed_with(agreed, step)
+                value = gate(value, from_partner[1], agreed)
+            if first and shift == 3:
+                for step in [bit for bit in bits if bit >= 2 * size_gy]:
+                    agreed = agreed_with(agreed, step)
+                value = gate(value, placed, agreed)
             from_partner[shift] = partner(value)
         out, _ = place(out, own=[arrived[1]], partner=[from_partner[1]])
         out, _ = place(out, own=[arrived[2]], partner=[])
         for shift in range(3, size_gx):
             out, placed = place(out, own=[arrived[shift]], partner=[from_partner[shift - 1]])
         out, _ = place(out, own=[], partner=[from_partner[size_gx - 1]])
-        return out, placed
-
-    out, token = round_of(None, 0)
+        return (out, agreed, placed) if first else out
+
+    out, agreed, token = round_of(None, 0)
     most_used = pl.pallas_call(
         most_kernel,
         in_specs=[VMEM, SMEM],
         out_specs=SMEM,
         out_shape=jax.ShapeDtypeStruct((1,), jnp.int32),
         cost_estimate=SMALL,
-    )(bounds, token)[0]
+    )(agreed, token)[0]
     for later in range(capacity, most, capacity):
-        out = lax.cond(most_used > later, lambda out: round_of(out, later)[0], lambda out: out, out)
+        out = lax.cond(most_used > later, lambda out: round_of(out, later), lambda out: out, out)
     return (
         out.reshape(SLOTS, 2 * home_count // 8, PACK, 8, LANES)
         .transpose(1, 3, 0, 2, 4)

time: 237 us -> 165 us (0.70)
  blocking collectives: 86 us -> 0 us
  starting transfers between devices: 9.89 us -> 21.4 us
  waiting for transfers between devices: 32.7 us -> 37.1 us
    all_gather x1 -> x0, blocking collectives: 86 us -> none  [body(): bounds = lax.all_gather(bound, axes, tiled=True)]
    ppermute x0 -> x5, waiting for transfers between devices: none -> 19 us  [agreed_with(): return jnp.maximum(value, lax.ppermute(value, axes, pairs))]
    ppermute x3, waiting for transfers between devices: 17 us -> 0.01 us  [across(): return lax.ppermute(value, 'gx', pairs)]
    ppermute x0 -> x5, starting transfers between devices: none -> 4.22 us  [agreed_with(): return jnp.maximum(value, lax.ppermute(value, axes, pairs))]
    ppermute x3, starting transfers between devices: 0.75 us -> 4.9 us  [partner(): return lax.ppermute(value, 'gy', pairs)]
    ppermute x1, starting transfers between devices: 0.07 us -> 2.73 us  [across_partner(): return lax.ppermute(value, axes, pairs)]
    ppermute x3, waiting for transfers between devices: 9.24 us -> 11.7 us  [partner(): return lax.ppermute(value, 'gy', pairs)]
  transfers between devices with their start and end apart: 9 -> 14, of which waited for: 3 -> 7; matrix products, arithmetic and copies ran while one was open for 0% -> 0% of each run, Pallas kernels for 35% -> 50%
where the time goes in v4:
time: 165 us
  Pallas kernels  103 us (62%)
  waiting for transfers between devices  37.1 us (22%)
  starting transfers between devices  21.4 us (13%)
  local copies, waits for them, and re-layouts  2.13 us (1%)
    pallas_call x4, Pallas kernels, bucket(): pl.pallas_call(functools.partial(bucket_kernel, shift, base, capacity, fi...  65 us
    pallas_call x5, Pallas kernels, placed_into(): pl.pallas_call(functools.partial(place_kernel, (len(own), len(partner)),...  30.3 us
    ppermute x5, waiting for transfers between devices, agreed_with(): return jnp.maximum(value, lax.ppermute(value, axes, pairs))  19 us
    ppermute x3, waiting for transfers between devices, partner(): return lax.ppermute(value, 'gy', pairs)  11.7 us
    ppermute x1, starting transfers between devices, body(): edge = lax.ppermute(back, axes, backward)  6.44 us
    ppermute x1, waiting for transfers between devices, body(): before = lax.ppermute(forth, axes, forward)  6.43 us
    ppermute x3, starting transfers between devices, partner(): return lax.ppermute(value, 'gy', pairs)  4.9 us
    ppermute x5, starting transfers between devices, agreed_with(): return jnp.maximum(value, lax.ppermute(value, axes, pairs))  4.22 us
  transfers between devices with their start and end apart: 14, of which 7 were waited for; matrix products, arithmetic and copies ran while one was open for 0% of the time, Pallas kernels for 50%

profile of v4, /device:TPU:0, one launch (start us, length us, event | category | flops | bytes accessed | tf_op | source)
XLA Modules:
  0.0 164.7 jit_solution(11108175600635821113)
XLA Ops:
  0.0 1.9 %shard_map.65 = (f32[520,128]{1,0:T(8,128)S(1)}, f32[256,128]{1,0:T(8,128)S(1)}) custom-call(s32[4,128]{1,0:T(4,128)} %bitcast.98, s32[4,128]{1,0:T(4,128)} %bitcast.88, s32[128]{0:T(128)} %aggregate_ref.11, f32[4096,128]{1,0:T(8,128)} %bitcast.73, f32[128,128,128]{2,1,0:T(8,128)} %bitcast.65), custom_call_target="tpu_custom_call" | custom-call | flops 1000000000 | bytes 3000000 | tf_op jit(solution)/shard_map/pallas_call | solution.py:465
  1.9 6.4 %collective-permute-start.12 = (f32[520,128]{1,0:T(8,128)S(1)}, f32[520,128]{1,0:T(8,128)S(1)}, u32[]{:S(2)}, u32[]{:S(2)}) collective-permute-start(f32[520,128]{1,0:T(8,128)S(1)} %get-tuple-element.56), channel_id=1, source_target_pairs={{0,31},{1,0},{2,1},{3,2},{4,3},{5,4},{6,5},{7,6},{8,7},{9,8},{10,9... | collective-permute-start | bytes 798728 | tf_op jit(solution)/shard_map/ppermute | solution.py:477
  8.3 0.0 collective-permute-start.13
  8.4 0.0 copy-done.9
  8.4 0.0 copy-start.8
  8.4 2.8 %shard_map.64 = (bf16[134,64,128]{2,1,0:T(8,128)(2,1)S(1)}, f32[8,128]{1,0:T(8,128)S(1)}) custom-call(s32[4,128]{1,0:T(4,128)S(1)} %bitcast.89, s32[128]{0:T(128)S(1)} %copy-done.9, s32[64]{0:T(128)S(1)} %copy-done.10, f32[4096,128]{1,0:T(8,128)S(1)} %bitcast.74), custom_call_target="tpu_custom_call" | custom-call | flops 5000000000 | bytes 15000000 | tf_op jit(solution)/shard_map/pallas_call | solution.py:481
  11.2 0.1 pad_add_fusion.me_ref.token_ref.other_ref
  11.3 6.4 %collective-permute-done.13.before_ref = f32[256,128]{1,0:T(8,128)S(1)} collective-permute-done((f32[256,128]{1,0:T(8,128)S(1)}, f32[256,128]{1,0:T(8,128)S(1)}, u32[]{:S(2)}, u32[]{:S(2)}) %collective-permute-start.13) | collective-permute-done | bytes 131104 | tf_op jit(solution)/shard_map/ppermute | solution.py:478
  17.7 0.0 collective-permute-done.12.edge_ref
  17.7 0.3 shard_map.66.w_ref
  18.0 2.1 %copy-done.5 = f32[128,4096]{1,0:T(8,128)S(1)} copy-done((f32[128,4096]{1,0:T(8,128)S(1)}, f32[128,4096]{1,0:T(8,128)}, u32[]{:S(2)}) %copy-start.5) | copy-done | bytes 2097176
  20.1 15.3 %shard_map.67.token_ref = f32[2440,128]{1,0:T(8,128)S(1)} custom-call(s32[3]{0:T(128)S(1)} %pad_add_fusion.me_ref.token_ref.other_ref, s32[4,128]{1,0:T(4,128)S(1)} %bitcast.99, s32[4,128]{1,0:T(4,128)S(1)} %bitcast.90, s32[128]{0:T(128)S(1)} %copy-done.9, s32[64]{0:T(128)S(1)} %copy-done.10, f32[128,128,128]{2,1,0:T(8,128)} %bitcast.66, ...), custom_call_target="tpu_custom_call" | custom-call | flops 1000000000 | bytes 3000000 | tf_op jit(solution)/shard_map/pallas_call | solution.py:506
  35.4 0.1 collective-permute-start.14
  35.5 17.7 %shard_map.68.token_ref = f32[2440,128]{1,0:T(8,128)S(1)} custom-call(s32[3]{0:T(128)S(1)} %pad_add_fusion.me_ref.token_ref.other_ref, s32[4,128]{1,0:T(4,128)S(1)} %bitcast.100, s32[4,128]{1,0:T(4,128)S(1)} %bitcast.91, s32[128]{0:T(128)S(1)} %copy-done.9, s32[64]{0:T(128)S(1)} %copy-done.10, f32[128,128,128]{2,1,0:T(8,128)S(1)} %bitcast.70, ...), custom_call_target="tpu_custom_call" | custom-call | flops 1000000000 | bytes 3000000 | tf_op jit(solution)/shard_map/pallas_call | solution.py:506
  53.2 2.2 %collective-permute-start.16 = (f32[2440,128]{1,0:T(8,128)S(1)}, f32[2440,128]{1,0:T(8,128)S(1)}, u32[]{:S(2)}, u32[]{:S(2)}) collective-permute-start(f32[2440,128]{1,0:T(8,128)S(1)} %shard_map.68.token_ref), channel_id=1, source_target_pairs={{0,16},{8,24},{16,0},{24,8},{1,17},{9,25},{17,1},{25,9},{2,18},{10... | collective-permute-start | bytes 3747848 | tf_op jit(solution)/shard_map/ppermute | solution.py:551
  55.5 14.4 %shard_map.69.value_ref = f32[2440,128]{1,0:T(8,128)S(1)} custom-call(s32[3]{0:T(128)S(1)} %pad_add_fusion.me_ref.token_ref.other_ref, s32[4,128]{1,0:T(4,128)S(1)} %bitcast.101, s32[4,128]{1,0:T(4,128)S(1)} %bitcast.92, s32[128]{0:T(128)S(1)} %copy-done.9, s32[64]{0:T(128)S(1)} %copy-done.10, f32[128,128,128]{2,1,0:T(8,128)S(1)} %bitcast.71, ...), custom_call_target="tpu_custom_call" | custom-call | flops 1000000000 | bytes 3000000 | tf_op jit(solution)/shard_map/pallas_call | solution.py:506
  69.9 0.0 collective-permute-done.14.token_ref
  69.9 0.1 shard_map.70.token_ref
  70.0 2.7 %collective-permute-start.17 = (f32[2440,128]{1,0:T(8,128)S(1)}, f32[2440,128]{1,0:T(8,128)S(1)}, u32[]{:S(2)}, u32[]{:S(2)}) collective-permute-start(f32[2440,128]{1,0:T(8,128)S(1)} %shard_map.70.token_ref), channel_id=1, source_target_pairs={{0,9},{1,8},{2,11},{3,10},{4,13},{5,12},{6,15},{7,14},{8,1},{9,0},... | collective-permute-start | bytes 3747848 | tf_op jit(solution)/shard_map/ppermute | solution.py:561
  72.7 17.6 %shard_map.71.refs_2_ = f32[2440,128]{1,0:T(8,128)S(1)} custom-call(s32[3]{0:T(128)S(1)} %pad_add_fusion.me_ref.token_ref.other_ref, s32[4,128]{1,0:T(4,128)S(1)} %bitcast.102, s32[4,128]{1,0:T(4,128)S(1)} %bitcast.93, s32[128]{0:T(128)S(1)} %copy-done.9, s32[64]{0:T(128)S(1)} %copy-done.10, f32[128,128,128]{2,1,0:T(8,128)S(1)} %bitcast.72, ...), custom_call_target="tpu_custom_call" | custom-call | flops 1000000000 | bytes 3000000 | tf_op jit(solution)/shard_map/pallas_call | solution.py:506
  90.3 0.9 collective-permute-start.15
  91.2 0.0 collective-permute-start.19
  91.2 0.0 collective-permute-start.7
  91.2 3.6 %collective-permute-done.7 = f32[8,128]{1,0:T(8,128)S(1)} collective-permute-done((f32[8,128]{1,0:T(8,128)S(1)}, f32[8,128]{1,0:T(8,128)S(1)}, u32[]{:S(2)}, u32[]{:S(2)}) %collective-permute-start.7) | collective-permute-done | bytes 4128 | tf_op jit(solution)/shard_map/ppermute | solution.py:567
  94.8 0.9 collective-permute-start.8
  95.7 3.6 %collective-permute-done.8 = f32[8,128]{1,0:T(8,128)S(1)} collective-permute-done((f32[8,128]{1,0:T(8,128)S(1)}, f32[8,128]{1,0:T(8,128)S(1)}, u32[]{:S(2)}, u32[]{:S(2)}) %collective-permute-start.8) | collective-permute-done | bytes 4128 | tf_op jit(solution)/shard_map/ppermute | solution.py:567
  99.3 0.0 collective-permute-start.9
  99.3 1.2 collective-permute-done.9
  100.5 2.2 %collective-permute-start.10 = (f32[8,128]{1,0:T(8,128)S(1)}, f32[8,128]{1,0:T(8,128)S(1)}, u32[]{:S(2)}, u32[]{:S(2)}) collective-permute-start(f32[8,128]{1,0:T(8,128)S(1)} %max.17), channel_id=1, source_target_pairs={{0,1},{1,0},{2,3},{3,2},{4,5},{5,4},{6,7},{7,6},{8,9},{9,8},{10,11... | collective-permute-start | bytes 12296 | tf_op jit(solution)/shard_map/ppermute | solution.py:567
  102.7 1.6 collective-permute-done.10
  104.3 1.2 collective-permute-start.11
  105.4 0.0 collective-permute-done.16.value_ref
  105.4 0.0 collective-permute-done.17.token_ref
  105.4 0.1 shard_map.72
  105.5 1.0 collective-permute-start.18
  106.5 9.0 %collective-permute-done.11 = f32[8,128]{1,0:T(8,128)S(1)} collective-permute-done((f32[8,128]{1,0:T(8,128)S(1)}, f32[8,128]{1,0:T(8,128)S(1)}, u32[]{:S(2)}, u32[]{:S(2)}) %collective-permute-start.11) | collective-permute-done | bytes 4128 | tf_op jit(solution)/shard_map/ppermute | solution.py:567
  115.5 10.5 %shard_map.73 = (f32[7,16,32,8,1,128]{5,4,3,2,1,0:T(1,128)}, s32[1]{0:T(128)}) custom-call(s32[3]{0:T(128)S(1)} %pad_add_fusion.me_ref.token_ref.other_ref, f32[2440,1,128]{2,1,0:T(1,128)S(1)} %bitcast.50, f32[2440,1,128]{2,1,0:T(1,128)S(1)} %bitcast.52, f32[2440,128]{1,0:T(8,128)S(1)} %shard_map.71.refs_2_), custom_call_target="tpu_custom_call" | custom-call | flops 1000000000 | bytes 3000000 | tf_op jit(solution)/shard_map/pallas_call | solution.py:403
  126.0 0.0 collective-permute-done.15.value_ref
  126.0 0.7 shard_map.78
  126.7 3.9 %collective-permute-start.20 = (f32[2440,128]{1,0:T(8,128)S(1)}, f32[2440,128]{1,0:T(8,128)S(1)}, u32[]{:S(2)}, u32[]{:S(2)}) collective-permute-start(f32[2440,128]{1,0:T(8,128)S(1)} %shard_map.78), channel_id=1, source_target_pairs={{0,1},{1,0},{2,3},{3,2},{4,5},{5,4},{6,7},{7,6},{8,9},{9,8},{10,11... | collective-permute-start | bytes 3747848 | tf_op jit(solution)/shard_map/ppermute | solution.py:555
  130.6 0.0 collective-permute-done.19
  130.6 5.7 %shard_map.74 = (f32[7,16,32,8,1,128]{5,4,3,2,1,0:T(1,128)}, s32[1]{0:T(128)}) custom-call(s32[3]{0:T(128)S(1)} %pad_add_fusion.me_ref.token_ref.other_ref, f32[2440,1,128]{2,1,0:T(1,128)S(1)} %bitcast.55, f32[2440,1,128]{2,1,0:T(1,128)S(1)} %bitcast.51, f32[7,16,32,8,1,128]{5,4,3,2,1,0:T(1,128)} %get-tuple-element.59.refs_2_), custom_call_target="tpu_custom_call", output_to_operand_aliasing={{0}: (3, {})} | custom-call | flops 1000000000 | bytes 3000000 | tf_op jit(solution)/shard_map/pallas_call | solution.py:403
  136.3 4.2 %shard_map.75 = (f32[7,16,32,8,1,128]{5,4,3,2,1,0:T(1,128)}, s32[1]{0:T(128)}) custom-call(s32[3]{0:T(128)S(1)} %pad_add_fusion.me_ref.token_ref.other_ref, f32[2440,1,128]{2,1,0:T(1,128)S(1)} %bitcast.53, f32[7,16,32,8,1,128]{5,4,3,2,1,0:T(1,128)} %get-tuple-element.60.refs_1_), custom_call_target="tpu_custom_call", output_to_operand_aliasing={{0}: (2, {})} | custom-call | flops 1000000000 | bytes 3000000 | tf_op jit(solution)/shard_map/pallas_call | solution.py:403
  140.5 0.0 collective-permute-done.18
  140.5 6.0 %shard_map.76 = (f32[7,16,32,8,1,128]{5,4,3,2,1,0:T(1,128)}, s32[1]{0:T(128)}) custom-call(s32[3]{0:T(128)S(1)} %pad_add_fusion.me_ref.token_ref.other_ref, f32[2440,1,128]{2,1,0:T(1,128)S(1)} %bitcast.54, f32[2440,1,128]{2,1,0:T(1,128)S(1)} %bitcast.57, f32[7,16,32,8,1,128]{5,4,3,2,1,0:T(1,128)} %get-tuple-element.61.refs_2_), custom_call_target="tpu_custom_call", output_to_operand_aliasing={{0}: (3, {})} | custom-call | flops 1000000000 | bytes 3000000 | tf_op jit(solution)/shard_map/pallas_call | solution.py:403
  146.5 1.9 %shard_map.77 = s32[1]{0:T(128)} custom-call(f32[8,128]{1,0:T(8,128)} %copy-done, s32[1]{0:T(128)} %get-tuple-element.62.token_ref), custom_call_target="tpu_custom_call" | custom-call | flops 1000000000 | bytes 3000000 | tf_op jit(solution)/shard_map/pallas_call | solution.py:608
  149.0 11.7 %collective-permute-done.20 = f32[2440,128]{1,0:T(8,128)S(1)} collective-permute-done((f32[2440,128]{1,0:T(8,128)S(1)}, f32[2440,128]{1,0:T(8,128)S(1)}, u32[]{:S(2)}, u32[]{:S(2)}) %collective-permute-start.20) | collective-permute-done | bytes 1249312 | tf_op jit(solution)/shard_map/ppermute | solution.py:555
  160.8 3.9 %shard_map.79 = (f32[7,16,32,8,1,128]{5,4,3,2,1,0:T(1,128)}, s32[1]{0:T(128)}) custom-call(s32[3]{0:T(128)S(1)} %pad_add_fusion.me_ref.token_ref.other_ref, f32[2440,1,128]{2,1,0:T(1,128)S(1)} %bitcast.64, f32[7,16,32,8,1,128]{5,4,3,2,1,0:T(1,128)} %get-tuple-element.64.refs_1_), custom_call_target="tpu_custom_call", output_to_operand_aliasing={{0}: (2, {})} | custom-call | flops 1000000000 | bytes 3000000 | tf_op jit(solution)/shard_map/pallas_call | solution.py:403
  (28 shorter events, 0.1 us)
Async XLA Ops:
  0.0 8.4 %copy-start.4 = (f32[128,4096]{1,0:T(8,128)S(1)}, f32[128,4096]{1,0:T(8,128)}, u32[]{:S(2)}) copy-start(f32[128,4096]{1,0:T(8,128)} %param.9) | copy-start | bytes 6291460
  0.0 8.4 %copy-start.7 = (s32[128,4]{0,1:T(4,128)S(1)}, s32[128,4]{0,1:T(4,128)}, u32[]{:S(2)}) copy-start(s32[128,4]{0,1:T(4,128)} %param.12) | copy-start | bytes 6148
  0.0 8.4 %copy-start.9 = (s32[128]{0:T(128)S(1)}, s32[128]{0:T(128)}, u32[]{:S(2)}) copy-start(s32[128]{0:T(128)} %aggregate_ref.11) | copy-start | bytes 1540
  0.0 8.4 %copy-start.10 = (s32[64]{0:T(128)S(1)}, s32[64]{0:T(128)}, u32[]{:S(2)}) copy-start(s32[64]{0:T(128)} %owner_ref.9) | copy-start | bytes 772
  1.9 15.8 %collective-permute-start.12 = (f32[520,128]{1,0:T(8,128)S(1)}, f32[520,128]{1,0:T(8,128)S(1)}, u32[]{:S(2)}, u32[]{:S(2)}) collective-permute-start(f32[520,128]{1,0:T(8,128)S(1)} %get-tuple-element.56), channel_id=1, source_target_pairs={{0,31},{1,0},{2,1},{3,2},{4,3},{5,4},{6,5},{7,6},{8,7},{9,8},{10,9... | collective-permute-start | bytes 798728 | tf_op jit(solution)/shard_map/ppermute | solution.py:477
  8.3 9.3 %collective-permute-start.13 = (f32[256,128]{1,0:T(8,128)S(1)}, f32[256,128]{1,0:T(8,128)S(1)}, u32[]{:S(2)}, u32[]{:S(2)}) collective-permute-start(f32[256,128]{1,0:T(8,128)S(1)} %get-tuple-element.57), channel_id=1, source_target_pairs={{0,1},{1,2},{2,3},{3,4},{4,5},{5,6},{6,7},{7,8},{8,9},{9,10},{10,1... | collective-permute-start | bytes 393224 | tf_op jit(solution)/shard_map/ppermute | solution.py:478
  8.4 9.6 %copy-start.8 = (s32[128,4]{0,1:T(4,128)S(1)}, s32[128,4]{0,1:T(4,128)}, u32[]{:S(2)}) copy-start(s32[128,4]{0,1:T(4,128)} %param.10) | copy-start | bytes 6148
  17.7 2.4 %copy-start.5 = (f32[128,4096]{1,0:T(8,128)S(1)}, f32[128,4096]{1,0:T(8,128)}, u32[]{:S(2)}) copy-start(f32[128,4096]{1,0:T(8,128)} %param.9) | copy-start | bytes 6291460
  17.7 17.8 %slice-start = ((s8[8388608]{0:T(1024)(128)(4,1)}), s8[4194304]{0:T(1024)(128)(4,1)S(1)}, s32[]{:S(2)}) async-start(s8[8388608]{0:T(1024)(128)(4,1)} %bitcast.68), calls=%async_computation | async-start | bytes 8388608
  18.0 54.7 %copy-start.2 = (bf16[134,64,128]{2,1,0:T(8,128)(2,1)}, bf16[134,64,128]{2,1,0:T(8,128)(2,1)S(1)}, u32[]{:S(2)}) copy-start(bf16[134,64,128]{2,1,0:T(8,128)(2,1)S(1)} %shard_map.66.w_ref) | copy-start | bytes 6586372
  20.1 15.4 %slice-start.1 = ((s8[8388608]{0:T(1024)(128)(4,1)}), s8[4194304]{0:T(1024)(128)(4,1)S(1)}, s32[]{:S(2)}) async-start(s8[8388608]{0:T(1024)(128)(4,1)} %bitcast.68), calls=%async_computation.1 | async-start | bytes 8388608
  35.4 34.5 %collective-permute-start.14 = (f32[2440,128]{1,0:T(8,128)S(1)}, f32[2440,128]{1,0:T(8,128)S(1)}, u32[]{:S(2)}, u32[]{:S(2)}) collective-permute-start(f32[2440,128]{1,0:T(8,128)S(1)} %shard_map.67.token_ref), channel_id=1, source_target_pairs={{0,1},{1,0},{2,3},{3,2},{4,5},{5,4},{6,7},{7,6},{8,9},{9,8},{10,11... | collective-permute-start | bytes 3747848 | tf_op jit(solution)/shard_map/ppermute | solution.py:555
  53.2 52.2 %collective-permute-start.16 = (f32[2440,128]{1,0:T(8,128)S(1)}, f32[2440,128]{1,0:T(8,128)S(1)}, u32[]{:S(2)}, u32[]{:S(2)}) collective-permute-start(f32[2440,128]{1,0:T(8,128)S(1)} %shard_map.68.token_ref), channel_id=1, source_target_pairs={{0,16},{8,24},{16,0},{24,8},{1,17},{9,25},{17,1},{25,9},{2,18},{10... | collective-permute-start | bytes 3747848 | tf_op jit(solution)/shard_map/ppermute | solution.py:551
  70.0 35.5 %collective-permute-start.17 = (f32[2440,128]{1,0:T(8,128)S(1)}, f32[2440,128]{1,0:T(8,128)S(1)}, u32[]{:S(2)}, u32[]{:S(2)}) collective-permute-start(f32[2440,128]{1,0:T(8,128)S(1)} %shard_map.70.token_ref), channel_id=1, source_target_pairs={{0,9},{1,8},{2,11},{3,10},{4,13},{5,12},{6,15},{7,14},{8,1},{9,0},... | collective-permute-start | bytes 3747848 | tf_op jit(solution)/shard_map/ppermute | solution.py:561
  90.3 35.6 %collective-permute-start.15 = (f32[2440,128]{1,0:T(8,128)S(1)}, f32[2440,128]{1,0:T(8,128)S(1)}, u32[]{:S(2)}, u32[]{:S(2)}) collective-permute-start(f32[2440,128]{1,0:T(8,128)S(1)} %shard_map.71.refs_2_), channel_id=1, source_target_pairs={{0,24},{8,16},{16,8},{24,0},{1,25},{9,17},{17,9},{25,1},{2,26},{10... | collective-permute-start | bytes 3747848 | tf_op jit(solution)/shard_map/ppermute | solution.py:551
  91.2 39.4 %collective-permute-start.19 = (f32[2440,128]{1,0:T(8,128)S(1)}, f32[2440,128]{1,0:T(8,128)S(1)}, u32[]{:S(2)}, u32[]{:S(2)}) collective-permute-start(f32[2440,128]{1,0:T(8,128)S(1)} %shard_map.70.token_ref), channel_id=1, source_target_pairs={{0,8},{8,0},{16,24},{24,16},{1,9},{9,1},{17,25},{25,17},{2,10},{10... | collective-permute-start | bytes 3747848 | tf_op jit(solution)/shard_map/ppermute | solution.py:551
  91.2 3.6 %collective-permute-start.7 = (f32[8,128]{1,0:T(8,128)S(1)}, f32[8,128]{1,0:T(8,128)S(1)}, u32[]{:S(2)}, u32[]{:S(2)}) collective-permute-start(f32[8,128]{1,0:T(8,128)S(1)} %get-tuple-element.55), channel_id=1, source_target_pairs={{0,2},{1,3},{2,0},{3,1},{4,6},{5,7},{6,4},{7,5},{8,10},{9,11},{10,... | collective-permute-start | bytes 12296 | tf_op jit(solution)/shard_map/ppermute | solution.py:567
  94.8 4.5 %collective-permute-start.8 = (f32[8,128]{1,0:T(8,128)S(1)}, f32[8,128]{1,0:T(8,128)S(1)}, u32[]{:S(2)}, u32[]{:S(2)}) collective-permute-start(f32[8,128]{1,0:T(8,128)S(1)} %max.15), channel_id=1, source_target_pairs={{0,4},{1,5},{2,6},{3,7},{4,0},{5,1},{6,2},{7,3},{8,12},{9,13},{10,... | collective-permute-start | bytes 12296 | tf_op jit(solution)/shard_map/ppermute | solution.py:567
  99.3 1.2 collective-permute-start.9
  100.5 3.7 %collective-permute-start.10 = (f32[8,128]{1,0:T(8,128)S(1)}, f32[8,128]{1,0:T(8,128)S(1)}, u32[]{:S(2)}, u32[]{:S(2)}) collective-permute-start(f32[8,128]{1,0:T(8,128)S(1)} %max.17), channel_id=1, source_target_pairs={{0,1},{1,0},{2,3},{3,2},{4,5},{5,4},{6,7},{7,6},{8,9},{9,8},{10,11... | collective-permute-start | bytes 12296 | tf_op jit(solution)/shard_map/ppermute | solution.py:567
  104.3 11.2 %collective-permute-start.11 = (f32[8,128]{1,0:T(8,128)S(1)}, f32[8,128]{1,0:T(8,128)S(1)}, u32[]{:S(2)}, u32[]{:S(2)}) collective-permute-start(f32[8,128]{1,0:T(8,128)S(1)} %max.18.other_ref), channel_id=1, source_target_pairs={{0,16},{1,17},{2,18},{3,19},{4,20},{5,21},{6,22},{7,23},{8,24},{9,... | collective-permute-start | bytes 12296 | tf_op jit(solution)/shard_map/ppermute | solution.py:567
  105.5 35.0 %collective-permute-start.18 = (f32[2440,128]{1,0:T(8,128)S(1)}, f32[2440,128]{1,0:T(8,128)S(1)}, u32[]{:S(2)}, u32[]{:S(2)}) collective-permute-start(f32[2440,128]{1,0:T(8,128)S(1)} %shard_map.72), channel_id=1, source_target_pairs={{0,1},{1,0},{2,3},{3,2},{4,5},{5,4},{6,7},{7,6},{8,9},{9,8},{10,11... | collective-permute-start | bytes 3747848 | tf_op jit(solution)/shard_map/ppermute | solution.py:555
  115.5 10.5 %copy-start = (f32[8,128]{1,0:T(8,128)}, f32[8,128]{1,0:T(8,128)S(1)}, u32[]{:S(2)}) copy-start(f32[8,128]{1,0:T(8,128)S(1)} %max.19.bounds_ref.other_ref) | copy-start | bytes 12292
  126.7 34.1 %collective-permute-start.20 = (f32[2440,128]{1,0:T(8,128)S(1)}, f32[2440,128]{1,0:T(8,128)S(1)}, u32[]{:S(2)}, u32[]{:S(2)}) collective-permute-start(f32[2440,128]{1,0:T(8,128)S(1)} %shard_map.78), channel_id=1, source_target_pairs={{0,1},{1,0},{2,3},{3,2},{4,5},{5,4},{6,7},{7,6},{8,9},{9,8},{10,11... | collective-permute-start | bytes 3747848 | tf_op jit(solution)/shard_map/ppermute | solution.py:555
  160.8 3.9 %copy-start.3 = (bf16[134,64,128]{2,1,0:T(8,128)(2,1)S(1)}, bf16[134,64,128]{2,1,0:T(8,128)(2,1)}, u32[]{:S(2)}) copy-start(bf16[134,64,128]{2,1,0:T(8,128)(2,1)} %copy-done.2) | copy-start | bytes 6586372
  160.8 3.9 %copy-start.6 = (f32[128,4096]{1,0:T(8,128)S(1)}, f32[128,4096]{1,0:T(8,128)}, u32[]{:S(2)}) copy-start(f32[128,4096]{1,0:T(8,128)} %param.9) | copy-start | bytes 6291460
